TPU v7x, 512 devices: a whole 4x4x16 slice. The times are simulated.
512 devices in a mesh: slab: 16 (over x, y), tile: 32 (over z, core).
Axes of the slice: x: 4, y: 4, z: 16, core: 2. Of those that a mesh axis runs over, the one named last changes fastest.
Arguments:
- slab_starts: float32 [16, 4, 8, 256, 512], P('slab', None, None, 'tile'), may hold values from -6 to 6
- substeps: int32 [16, 32], P('slab', 'tile'), may hold values from 2 to 6
- east_velocity: float32 [8, 256, 512], P(None, 'tile'), may hold values from -0.3 to 0.3
- north_velocity: float32 [8, 256, 512], P(None, 'tile'), may hold values from -0.3 to 0.3
- diffusivity: float32 [8, 256, 512], P(None, 'tile'), may hold values from 0.01 to 0.1
Outputs:
- updated: float32 [16, 4, 8, 256, 512], P('slab', None, None, 'tile')
All inputs are finite; a program needn't handle non-finite values.
Results may differ from a plain program's by a relative error of at most 0.0003.
Values sent between devices are 32-bit elements; how exact they have to be, the bound alone decides.
No kernel may reach another device: no remote copies, remote signals or barrier semaphores. Data moves between devices by JAX's collectives and lax.ppermute only.
A program may use at most 64 MiB of HBM per device.

v0:
```python
import jax
import jax.numpy as jnp
from jax import lax
from jax.sharding import PartitionSpec as P

MAXSUB = 6


def with_halo(block, sides, width):
    for axis, dim in sides:
        count = lax.axis_size(axis)
        forward = [(i, i + 1) for i in range(count - 1)]
        backward = [(target, source) for source, target in forward]
        low = lax.ppermute(
            lax.slice_in_dim(block, block.shape[dim] - width, None, axis=dim), axis, forward
        )
        high = lax.ppermute(lax.slice_in_dim(block, 0, width, axis=dim), axis, backward)
        block = jnp.concatenate([low, block, high], axis=dim)
    return block


def from_behind(block, axis, distance):
    devices = range(lax.axis_size(axis))
    route = [(i - distance, i) for i in devices if i - distance in devices]
    return lax.ppermute(block, axis, route)


def minmod(first_slope, second_slope):
    return (
        0.5
        * (jnp.sign(first_slope) + jnp.sign(second_slope))
        * jnp.minimum(jnp.abs(first_slope), jnp.abs(second_slope))
    )


def face_flux(behind, upwind, downwind, beyond, velocity, fraction):
    limiter = 0.5 * (1.0 - jnp.abs(velocity) * fraction)
    west_value = upwind + limiter * minmod(downwind - upwind, upwind - behind)
    east_value = downwind - limiter * minmod(beyond - downwind, downwind - upwind)
    return jnp.maximum(velocity, 0.0) * west_value + jnp.minimum(velocity, 0.0) * east_value


def fine_step(window, east_faces, north_faces, diffusivity, fraction):
    cells_x = diffusivity.shape[1]
    cells_y = diffusivity.shape[2]
    inner = window[:, :, :, 2 : cells_y + 2]
    flux_across = face_flux(
        inner[:, :, 0 : cells_x + 1],
        inner[:, :, 1 : cells_x + 2],
        inner[:, :, 2 : cells_x + 3],
        inner[:, :, 3 : cells_x + 4],
        east_faces,
        fraction,
    )
    inner = window[:, :, 2 : cells_x + 2, :]
    flux_along = face_flux(
        inner[..., 0 : cells_y + 1],
        inner[..., 1 : cells_y + 2],
        inner[..., 2 : cells_y + 3],
        inner[..., 3 : cells_y + 4],
        north_faces,
        fraction,
    )
    center = window[:, :, 2 : cells_x + 2, 2 : cells_y + 2]
    laplace = (
        window[:, :, 1 : cells_x + 1, 2 : cells_y + 2]
        + window[:, :, 3 : cells_x + 3, 2 : cells_y + 2]
        + window[:, :, 2 : cells_x + 2, 1 : cells_y + 1]
        + window[:, :, 2 : cells_x + 2, 3 : cells_y + 3]
        - 4.0 * center
    )
    rate = (
        -(flux_across[:, :, 1:] - flux_across[:, :, :-1])
        - (flux_along[..., 1:] - flux_along[..., :-1])
        + diffusivity * laplace
    )
    return center + fraction * rate


def coarse_step(padded, east_faces, north_faces, diffusivity):
    cells_x = diffusivity.shape[1]
    cells_y = diffusivity.shape[2]
    flux_across = (
        jnp.maximum(east_faces, 0.0) * padded[:, :, 0 : cells_x + 1, 1 : cells_y + 1]
        + jnp.minimum(east_faces, 0.0) * padded[:, :, 1 : cells_x + 2, 1 : cells_y + 1]
    )
    flux_along = (
        jnp.maximum(north_faces, 0.0) * padded[:, :, 1 : cells_x + 1, 0 : cells_y + 1]
        + jnp.minimum(north_faces, 0.0) * padded[:, :, 1 : cells_x + 1, 1 : cells_y + 2]
    )
    center = padded[:, :, 1 : cells_x + 1, 1 : cells_y + 1]
    laplace = (
        padded[:, :, 0:cells_x, 1 : cells_y + 1]
        + padded[:, :, 2 : cells_x + 2, 1 : cells_y + 1]
        + padded[:, :, 1 : cells_x + 1, 0:cells_y]
        + padded[:, :, 1 : cells_x + 1, 2 : cells_y + 2]
        - 4.0 * center
    )
    return (
        center
        - (flux_across[:, :, 1:] - flux_across[:, :, :-1])
        - (flux_along[..., 1:] - flux_along[..., :-1])
        + diffusivity * laplace
    )


def pad_along(field, margin):
    return jnp.pad(field, ((0, 0), (0, 0), (0, 0), (margin, margin)))


def fine_window(field):
    return pad_along(with_halo(field, (("tile", 2),), 2), 2)


def chain_window(field):
    return pad_along(with_halo(field, (("tile", 2),), 1), 1)


def run_chain(initial, difference, coarse_of, block_dim):
    slab_count = lax.axis_size("slab")
    slab_index = lax.axis_index("slab")
    first_slab = slab_index == 0
    whole_width = initial.shape[block_dim]
    zero_offset = jnp.zeros((), jnp.int32)

    def advance(current, unused):
        proposal = coarse_of(current, zero_offset, whole_width) + difference
        arrived = from_behind(proposal, "slab", 1)
        return (jnp.where(first_slab, initial, arrived), None)

    current, _ = lax.scan(advance, initial, None, length=slab_count - 1)
    result = coarse_of(current, zero_offset, whole_width) + difference
    return result


def on_device(slab_starts, substeps, east_velocity, north_velocity, diffusivity):
    initial = slab_starts[0]
    levels, cells_x, cells_y = diffusivity.shape
    west_row = from_behind(east_velocity[:, -1:, :], "tile", 1)
    east_faces = jnp.concatenate([west_row, east_velocity], axis=1)
    north_faces = jnp.concatenate(
        [jnp.zeros((levels, cells_x, 1), north_velocity.dtype), north_velocity], axis=2
    )
    step_count = substeps[0, 0]
    fraction = 1.0 / step_count.astype(jnp.float32)
    field = initial
    for substep in range(MAXSUB):
        window = fine_window(field)
        stepped = fine_step(window, east_faces, north_faces, diffusivity, fraction)
        field = jnp.where(substep < step_count, stepped, field)
    old_padded = pad_along(with_halo(initial, (("tile", 2),), 1), 1)
    previous = coarse_step(old_padded, east_faces, north_faces, diffusivity)
    difference = field - previous

    def coarse_tiles(portion, offset, width):
        return coarse_step(chain_window(portion), east_faces, north_faces, diffusivity)

    result = run_chain(initial, difference, coarse_tiles, 0)
    return result[None]


def solution(mesh):
    return jax.shard_map(
        on_device,
        mesh=mesh,
        in_specs=(
            P("slab", None, None, "tile", None),
            P("slab", "tile"),
            P(None, "tile", None),
            P(None, "tile", None),
            P(None, "tile", None),
        ),
        out_specs=P("slab", None, None, "tile", None),
        check_vma=False,
    )
```

profile of v0, /device:TPU:194, one launch (start us, length us, event | category | flops | bytes accessed | tf_op | source)
XLA Modules:
  0.0 601.1 jit_solution(3562401629483936953)
XLA Ops:
  4.3 3.9 collective-permute-start.4
  11.5 2.4 collective-permute-start.16
  15.7 3.2 collective-permute-start.17
  21.1 3.0 fusion.55
  24.8 4.8 collective-permute-start.6
  31.6 2.5 collective-permute-done.7
  38.5 6.2 %collective-permute-start.8 = (f32[4,8,2,512]{3,2,1,0:T(2,128)S(1)}, f32[4,8,2,512]{3,2,1,0:T(2,128)S(1)}, u32[]{:S(2)}, u32[]{:S(2)}) collective-permute-start(f32[4,8,2,512]{3,2,1,0:T(2,128)S(1)} %get-tuple-element.141), channel_id=1, source_target_pairs={{0,1},{1,2},{2,3},{3,4},{4,5},{5,6},{6,7},{7,8},{8,9},{9,10},{10,1... | collective-permute-start | bytes 393224 | tf_op jit(solution)/shard_map/ppermute | solution.py:14
  44.7 12.0 %collective-permute-start.9 = (f32[4,8,2,512]{3,2,1,0:T(2,128)S(1)}, f32[4,8,2,512]{3,2,1,0:T(2,128)S(1)}, u32[]{:S(2)}, u32[]{:S(2)}) collective-permute-start(f32[4,8,2,512]{3,2,1,0:T(2,128)S(1)} %get-tuple-element.142), channel_id=1, source_target_pairs={{1,0},{2,1},{3,2},{4,3},{5,4},{6,5},{7,6},{8,7},{9,8},{10,9},{11,1... | collective-permute-start | bytes 393224 | tf_op jit(solution)/shard_map/ppermute | solution.py:17
  61.2 2.4 collective-permute-start.10
  63.6 3.2 collective-permute-start.11
  74.4 5.2 collective-permute-start.12
  81.6 2.8 collective-permute-done.13
  87.2 2.8 multiply_add_fusion.1
  91.7 6.2 %collective-permute-start.14 = (f32[4,8,2,512]{3,2,1,0:T(2,128)S(1)}, f32[4,8,2,512]{3,2,1,0:T(2,128)S(1)}, u32[]{:S(2)}, u32[]{:S(2)}) collective-permute-start(f32[4,8,2,512]{3,2,1,0:T(2,128)S(1)} %get-tuple-element.133), channel_id=1, source_target_pairs={{0,1},{1,2},{2,3},{3,4},{4,5},{5,6},{6,7},{7,8},{8,9},{9,10},{10,1... | collective-permute-start | bytes 393224 | tf_op jit(solution)/shard_map/ppermute | solution.py:14
  108.2 478.4 %while.12 = (s32[]{:T(128)}, f32[4,8,8,512]{3,2,1,0:T(8,128)S(1)}, pred[]{:T(512)}, f32[8,9,512]{2,1,0:T(8,128)S(1)}, f32[8,8,513]{2,1,0:T(8,128)S(1)}, /*index=...) while((s32[]{:T(128)}, f32[4,8,8,512]{3,2,1,0:T(8,128)S(1)}, ...), condition=%wide.region_1.2_spmd, body=%wide.region_0.1_spmd.sunk | while | flops 4274050 | bytes 24864016 | solution.py:131
  108.3 3.8 collective-permute-start.1
  112.1 3.1 collective-permute-start
  123.8 3.6 collective-permute-start.2
  127.4 15.1 %collective-permute-done.2 = f32[4,8,8,512]{3,2,1,0:T(8,128)S(1)} collective-permute-done((f32[4,8,8,512]{3,2,1,0:T(8,128)}, f32[4,8,8,512]{3,2,1,0:T(8,128)S(1)}, u32[]{:S(2)}, u32[]{:S(2)}) %collective-permute-start.2) | collective-permute-done | bytes 524320 | tf_op jit(solution)/shard_map/while/body/eval_jaxpr/ppermute | solution.py:25
  144.8 2.4 collective-permute-start
  158.6 16.3 %collective-permute-done.2 = f32[4,8,8,512]{3,2,1,0:T(8,128)S(1)} collective-permute-done((f32[4,8,8,512]{3,2,1,0:T(8,128)}, f32[4,8,8,512]{3,2,1,0:T(8,128)S(1)}, u32[]{:S(2)}, u32[]{:S(2)}) %collective-permute-start.2) | collective-permute-done | bytes 524320 | tf_op jit(solution)/shard_map/while/body/eval_jaxpr/ppermute | solution.py:25
  177.0 2.4 collective-permute-start
  190.9 16.8 %collective-permute-done.2 = f32[4,8,8,512]{3,2,1,0:T(8,128)S(1)} collective-permute-done((f32[4,8,8,512]{3,2,1,0:T(8,128)}, f32[4,8,8,512]{3,2,1,0:T(8,128)S(1)}, u32[]{:S(2)}, u32[]{:S(2)}) %collective-permute-start.2) | collective-permute-done | bytes 524320 | tf_op jit(solution)/shard_map/while/body/eval_jaxpr/ppermute | solution.py:25
  209.9 2.4 collective-permute-start
  223.7 16.8 %collective-permute-done.2 = f32[4,8,8,512]{3,2,1,0:T(8,128)S(1)} collective-permute-done((f32[4,8,8,512]{3,2,1,0:T(8,128)}, f32[4,8,8,512]{3,2,1,0:T(8,128)S(1)}, u32[]{:S(2)}, u32[]{:S(2)}) %collective-permute-start.2) | collective-permute-done | bytes 524320 | tf_op jit(solution)/shard_map/while/body/eval_jaxpr/ppermute | solution.py:25
  242.7 2.4 collective-permute-start
  256.5 16.6 %collective-permute-done.2 = f32[4,8,8,512]{3,2,1,0:T(8,128)S(1)} collective-permute-done((f32[4,8,8,512]{3,2,1,0:T(8,128)}, f32[4,8,8,512]{3,2,1,0:T(8,128)S(1)}, u32[]{:S(2)}, u32[]{:S(2)}) %collective-permute-start.2) | collective-permute-done | bytes 524320 | tf_op jit(solution)/shard_map/while/body/eval_jaxpr/ppermute | solution.py:25
  275.2 2.4 collective-permute-start
  289.1 16.3 %collective-permute-done.2 = f32[4,8,8,512]{3,2,1,0:T(8,128)S(1)} collective-permute-done((f32[4,8,8,512]{3,2,1,0:T(8,128)}, f32[4,8,8,512]{3,2,1,0:T(8,128)S(1)}, u32[]{:S(2)}, u32[]{:S(2)}) %collective-permute-start.2) | collective-permute-done | bytes 524320 | tf_op jit(solution)/shard_map/while/body/eval_jaxpr/ppermute | solution.py:25
  307.6 2.4 collective-permute-start
  321.4 16.1 %collective-permute-done.2 = f32[4,8,8,512]{3,2,1,0:T(8,128)S(1)} collective-permute-done((f32[4,8,8,512]{3,2,1,0:T(8,128)}, f32[4,8,8,512]{3,2,1,0:T(8,128)S(1)}, u32[]{:S(2)}, u32[]{:S(2)}) %collective-permute-start.2) | collective-permute-done | bytes 524320 | tf_op jit(solution)/shard_map/while/body/eval_jaxpr/ppermute | solution.py:25
  339.7 2.4 collective-permute-start
  353.5 15.8 %collective-permute-done.2 = f32[4,8,8,512]{3,2,1,0:T(8,128)S(1)} collective-permute-done((f32[4,8,8,512]{3,2,1,0:T(8,128)}, f32[4,8,8,512]{3,2,1,0:T(8,128)S(1)}, u32[]{:S(2)}, u32[]{:S(2)}) %collective-permute-start.2) | collective-permute-done | bytes 524320 | tf_op jit(solution)/shard_map/while/body/eval_jaxpr/ppermute | solution.py:25
  371.5 2.4 collective-permute-start
  385.3 15.5 %collective-permute-done.2 = f32[4,8,8,512]{3,2,1,0:T(8,128)S(1)} collective-permute-done((f32[4,8,8,512]{3,2,1,0:T(8,128)}, f32[4,8,8,512]{3,2,1,0:T(8,128)S(1)}, u32[]{:S(2)}, u32[]{:S(2)}) %collective-permute-start.2) | collective-permute-done | bytes 524320 | tf_op jit(solution)/shard_map/while/body/eval_jaxpr/ppermute | solution.py:25
  403.1 2.4 collective-permute-start
  416.9 15.2 %collective-permute-done.2 = f32[4,8,8,512]{3,2,1,0:T(8,128)S(1)} collective-permute-done((f32[4,8,8,512]{3,2,1,0:T(8,128)}, f32[4,8,8,512]{3,2,1,0:T(8,128)S(1)}, u32[]{:S(2)}, u32[]{:S(2)}) %collective-permute-start.2) | collective-permute-done | bytes 524320 | tf_op jit(solution)/shard_map/while/body/eval_jaxpr/ppermute | solution.py:25
  434.3 2.4 collective-permute-start
  448.1 14.9 %collective-permute-done.2 = f32[4,8,8,512]{3,2,1,0:T(8,128)S(1)} collective-permute-done((f32[4,8,8,512]{3,2,1,0:T(8,128)}, f32[4,8,8,512]{3,2,1,0:T(8,128)S(1)}, u32[]{:S(2)}, u32[]{:S(2)}) %collective-permute-start.2) | collective-permute-done | bytes 524320 | tf_op jit(solution)/shard_map/while/body/eval_jaxpr/ppermute | solution.py:25
  465.1 2.4 collective-permute-start
  478.9 14.5 %collective-permute-done.2 = f32[4,8,8,512]{3,2,1,0:T(8,128)S(1)} collective-permute-done((f32[4,8,8,512]{3,2,1,0:T(8,128)}, f32[4,8,8,512]{3,2,1,0:T(8,128)S(1)}, u32[]{:S(2)}, u32[]{:S(2)}) %collective-permute-start.2) | collective-permute-done | bytes 524320 | tf_op jit(solution)/shard_map/while/body/eval_jaxpr/ppermute | solution.py:25
  495.6 2.4 collective-permute-start
  509.4 15.0 %collective-permute-done.2 = f32[4,8,8,512]{3,2,1,0:T(8,128)S(1)} collective-permute-done((f32[4,8,8,512]{3,2,1,0:T(8,128)}, f32[4,8,8,512]{3,2,1,0:T(8,128)S(1)}, u32[]{:S(2)}, u32[]{:S(2)}) %collective-permute-start.2) | collective-permute-done | bytes 524320 | tf_op jit(solution)/shard_map/while/body/eval_jaxpr/ppermute | solution.py:25
  526.6 2.4 collective-permute-start
  540.4 15.2 %collective-permute-done.2 = f32[4,8,8,512]{3,2,1,0:T(8,128)S(1)} collective-permute-done((f32[4,8,8,512]{3,2,1,0:T(8,128)}, f32[4,8,8,512]{3,2,1,0:T(8,128)S(1)}, u32[]{:S(2)}, u32[]{:S(2)}) %collective-permute-start.2) | collective-permute-done | bytes 524320 | tf_op jit(solution)/shard_map/while/body/eval_jaxpr/ppermute | solution.py:25
  557.8 2.4 collective-permute-start
  571.6 14.9 %collective-permute-done.2 = f32[4,8,8,512]{3,2,1,0:T(8,128)S(1)} collective-permute-done((f32[4,8,8,512]{3,2,1,0:T(8,128)}, f32[4,8,8,512]{3,2,1,0:T(8,128)S(1)}, u32[]{:S(2)}, u32[]{:S(2)}) %collective-permute-start.2) | collective-permute-done | bytes 524320 | tf_op jit(solution)/shard_map/while/body/eval_jaxpr/ppermute | solution.py:25
  588.7 2.5 collective-permute-start.18
  (606 shorter events, 253.7 us)
Async XLA Ops:
  1.0 17.8 %collective-permute-start.3 = (f32[8,1,512]{2,1,0:T(1,128)S(1)}, f32[8,1,512]{2,1,0:T(1,128)S(1)}, u32[]{:S(2)}, u32[]{:S(2)}) collective-permute-start(f32[8,1,512]{2,1,0:T(1,128)S(1)} %slice.603), channel_id=1, source_target_pairs={{0,1},{1,2},{2,3},{3,4},{4,5},{5,6},{6,7},{7,8},{8,9},{9,10},{10,1... | collective-permute-start | bytes 49160 | tf_op jit(solution)/shard_map/ppermute | solution.py:25
  4.3 14.7 %collective-permute-start.4 = (f32[4,8,2,512]{3,2,1,0:T(2,128)S(1)}, f32[4,8,2,512]{3,2,1,0:T(2,128)S(1)}, u32[]{:S(2)}, u32[]{:S(2)}) collective-permute-start(f32[4,8,2,512]{3,2,1,0:T(2,128)S(1)} %get-tuple-element.145), channel_id=1, source_target_pairs={{0,1},{1,2},{2,3},{3,4},{4,5},{5,6},{6,7},{7,8},{8,9},{9,10},{10,1... | collective-permute-start | bytes 393224 | tf_op jit(solution)/shard_map/ppermute | solution.py:14
  8.2 10.8 %collective-permute-start.5 = (f32[4,8,2,512]{3,2,1,0:T(2,128)S(1)}, f32[4,8,2,512]{3,2,1,0:T(2,128)S(1)}, u32[]{:S(2)}, u32[]{:S(2)}) collective-permute-start(f32[4,8,2,512]{3,2,1,0:T(2,128)S(1)} %get-tuple-element.146), channel_id=1, source_target_pairs={{1,0},{2,1},{3,2},{4,3},{5,4},{6,5},{7,6},{8,7},{9,8},{10,9},{11,1... | collective-permute-start | bytes 393224 | tf_op jit(solution)/shard_map/ppermute | solution.py:17
  11.5 9.5 %collective-permute-start.16 = (f32[4,8,1,512]{3,2,1,0:T(1,128)S(1)}, f32[4,8,1,512]{3,2,1,0:T(1,128)S(1)}, u32[]{:S(2)}, u32[]{:S(2)}) collective-permute-start(f32[4,8,1,512]{3,2,1,0:T(1,128)S(1)} %get-tuple-element.135), channel_id=1, source_target_pairs={{0,1},{1,2},{2,3},{3,4},{4,5},{5,6},{6,7},{7,8},{8,9},{9,10},{10,1... | collective-permute-start | bytes 196616 | tf_op jit(solution)/shard_map/ppermute | solution.py:14
  15.7 5.4 collective-permute-start.17
  24.8 6.8 %collective-permute-start.6 = (f32[4,8,2,512]{3,2,1,0:T(2,128)S(1)}, f32[4,8,2,512]{3,2,1,0:T(2,128)S(1)}, u32[]{:S(2)}, u32[]{:S(2)}) collective-permute-start(f32[4,8,2,512]{3,2,1,0:T(2,128)S(1)} %get-tuple-element.143), channel_id=1, source_target_pairs={{0,1},{1,2},{2,3},{3,4},{4,5},{5,6},{6,7},{7,8},{8,9},{9,10},{10,1... | collective-permute-start | bytes 393224 | tf_op jit(solution)/shard_map/ppermute | solution.py:14
  38.5 18.2 %collective-permute-start.8 = (f32[4,8,2,512]{3,2,1,0:T(2,128)S(1)}, f32[4,8,2,512]{3,2,1,0:T(2,128)S(1)}, u32[]{:S(2)}, u32[]{:S(2)}) collective-permute-start(f32[4,8,2,512]{3,2,1,0:T(2,128)S(1)} %get-tuple-element.141), channel_id=1, source_target_pairs={{0,1},{1,2},{2,3},{3,4},{4,5},{5,6},{6,7},{7,8},{8,9},{9,10},{10,1... | collective-permute-start | bytes 393224 | tf_op jit(solution)/shard_map/ppermute | solution.py:14
  44.7 12.0 %collective-permute-start.9 = (f32[4,8,2,512]{3,2,1,0:T(2,128)S(1)}, f32[4,8,2,512]{3,2,1,0:T(2,128)S(1)}, u32[]{:S(2)}, u32[]{:S(2)}) collective-permute-start(f32[4,8,2,512]{3,2,1,0:T(2,128)S(1)} %get-tuple-element.142), channel_id=1, source_target_pairs={{1,0},{2,1},{3,2},{4,3},{5,4},{6,5},{7,6},{8,7},{9,8},{10,9},{11,1... | collective-permute-start | bytes 393224 | tf_op jit(solution)/shard_map/ppermute | solution.py:17
  61.2 6.3 %collective-permute-start.10 = (f32[4,8,2,512]{3,2,1,0:T(2,128)S(1)}, f32[4,8,2,512]{3,2,1,0:T(2,128)S(1)}, u32[]{:S(2)}, u32[]{:S(2)}) collective-permute-start(f32[4,8,2,512]{3,2,1,0:T(2,128)S(1)} %get-tuple-element.139), channel_id=1, source_target_pairs={{0,1},{1,2},{2,3},{3,4},{4,5},{5,6},{6,7},{7,8},{8,9},{9,10},{10,1... | collective-permute-start | bytes 393224 | tf_op jit(solution)/shard_map/ppermute | solution.py:14
  63.6 5.7 collective-permute-start.11
  74.4 7.2 %collective-permute-start.12 = (f32[4,8,2,512]{3,2,1,0:T(2,128)}, f32[4,8,2,512]{3,2,1,0:T(2,128)S(1)}, u32[]{:S(2)}, u32[]{:S(2)}) collective-permute-start(f32[4,8,2,512]{3,2,1,0:T(2,128)} %get-tuple-element.137), channel_id=1, source_target_pairs={{0,1},{1,2},{2,3},{3,4},{4,5},{5,6},{6,7},{7,8},{8,9},{9,10},{10,1... | collective-permute-start | bytes 393224 | tf_op jit(solution)/shard_map/ppermute | solution.py:14
  91.7 9.2 %collective-permute-start.14 = (f32[4,8,2,512]{3,2,1,0:T(2,128)S(1)}, f32[4,8,2,512]{3,2,1,0:T(2,128)S(1)}, u32[]{:S(2)}, u32[]{:S(2)}) collective-permute-start(f32[4,8,2,512]{3,2,1,0:T(2,128)S(1)} %get-tuple-element.133), channel_id=1, source_target_pairs={{0,1},{1,2},{2,3},{3,4},{4,5},{5,6},{6,7},{7,8},{8,9},{9,10},{10,1... | collective-permute-start | bytes 393224 | tf_op jit(solution)/shard_map/ppermute | solution.py:14
  108.3 7.9 %collective-permute-start.1 = (f32[4,8,1,512]{3,2,1,0:T(1,128)S(1)}, f32[4,8,1,512]{3,2,1,0:T(1,128)S(1)}, u32[]{:S(2)}, u32[]{:S(2)}) collective-permute-start(f32[4,8,1,512]{3,2,1,0:T(1,128)S(1)} %get-tuple-element.213), channel_id=1, source_target_pairs={{1,0},{2,1},{3,2},{4,3},{5,4},{6,5},{7,6},{8,7},{9,8},{10,9},{11,1... | collective-permute-start | bytes 196616 | tf_op jit(solution)/shard_map/while/body/eval_jaxpr/ppermute | solution.py:17
  112.1 5.6 collective-permute-start
  123.8 18.8 %collective-permute-start.2 = (f32[4,8,8,512]{3,2,1,0:T(8,128)}, f32[4,8,8,512]{3,2,1,0:T(8,128)S(1)}, u32[]{:S(2)}, u32[]{:S(2)}) collective-permute-start(f32[4,8,8,512]{3,2,1,0:T(8,128)} %fusion.140), channel_id=1, source_target_pairs={{0,32},{32,64},{64,96},{96,128},{128,160},{160,192},{192,224},{224... | collective-permute-start | bytes 1572872 | tf_op jit(solution)/shard_map/while/body/eval_jaxpr/ppermute | solution.py:25
  142.8 5.3 collective-permute-start.1
  144.8 5.6 collective-permute-start
  156.5 18.3 %collective-permute-start.2 = (f32[4,8,8,512]{3,2,1,0:T(8,128)}, f32[4,8,8,512]{3,2,1,0:T(8,128)S(1)}, u32[]{:S(2)}, u32[]{:S(2)}) collective-permute-start(f32[4,8,8,512]{3,2,1,0:T(8,128)} %fusion.140), channel_id=1, source_target_pairs={{0,32},{32,64},{64,96},{96,128},{128,160},{160,192},{192,224},{224... | collective-permute-start | bytes 1572872 | tf_op jit(solution)/shard_map/while/body/eval_jaxpr/ppermute | solution.py:25
  175.1 5.3 collective-permute-start.1
  177.0 5.6 collective-permute-start
  188.8 18.9 %collective-permute-start.2 = (f32[4,8,8,512]{3,2,1,0:T(8,128)}, f32[4,8,8,512]{3,2,1,0:T(8,128)S(1)}, u32[]{:S(2)}, u32[]{:S(2)}) collective-permute-start(f32[4,8,8,512]{3,2,1,0:T(8,128)} %fusion.140), channel_id=1, source_target_pairs={{0,32},{32,64},{64,96},{96,128},{128,160},{160,192},{192,224},{224... | collective-permute-start | bytes 1572872 | tf_op jit(solution)/shard_map/while/body/eval_jaxpr/ppermute | solution.py:25
  207.9 5.3 collective-permute-start.1
  209.9 5.6 collective-permute-start
  221.6 18.9 %collective-permute-start.2 = (f32[4,8,8,512]{3,2,1,0:T(8,128)}, f32[4,8,8,512]{3,2,1,0:T(8,128)S(1)}, u32[]{:S(2)}, u32[]{:S(2)}) collective-permute-start(f32[4,8,8,512]{3,2,1,0:T(8,128)} %fusion.140), channel_id=1, source_target_pairs={{0,32},{32,64},{64,96},{96,128},{128,160},{160,192},{192,224},{224... | collective-permute-start | bytes 1572872 | tf_op jit(solution)/shard_map/while/body/eval_jaxpr/ppermute | solution.py:25
  242.7 5.6 collective-permute-start
  254.4 18.6 %collective-permute-start.2 = (f32[4,8,8,512]{3,2,1,0:T(8,128)}, f32[4,8,8,512]{3,2,1,0:T(8,128)S(1)}, u32[]{:S(2)}, u32[]{:S(2)}) collective-permute-start(f32[4,8,8,512]{3,2,1,0:T(8,128)} %fusion.140), channel_id=1, source_target_pairs={{0,32},{32,64},{64,96},{96,128},{128,160},{160,192},{192,224},{224... | collective-permute-start | bytes 1572872 | tf_op jit(solution)/shard_map/while/body/eval_jaxpr/ppermute | solution.py:25
  275.2 5.6 collective-permute-start
  287.0 18.4 %collective-permute-start.2 = (f32[4,8,8,512]{3,2,1,0:T(8,128)}, f32[4,8,8,512]{3,2,1,0:T(8,128)S(1)}, u32[]{:S(2)}, u32[]{:S(2)}) collective-permute-start(f32[4,8,8,512]{3,2,1,0:T(8,128)} %fusion.140), channel_id=1, source_target_pairs={{0,32},{32,64},{64,96},{96,128},{128,160},{160,192},{192,224},{224... | collective-permute-start | bytes 1572872 | tf_op jit(solution)/shard_map/while/body/eval_jaxpr/ppermute | solution.py:25
  307.6 5.6 collective-permute-start
  319.3 18.2 %collective-permute-start.2 = (f32[4,8,8,512]{3,2,1,0:T(8,128)}, f32[4,8,8,512]{3,2,1,0:T(8,128)S(1)}, u32[]{:S(2)}, u32[]{:S(2)}) collective-permute-start(f32[4,8,8,512]{3,2,1,0:T(8,128)} %fusion.140), channel_id=1, source_target_pairs={{0,32},{32,64},{64,96},{96,128},{128,160},{160,192},{192,224},{224... | collective-permute-start | bytes 1572872 | tf_op jit(solution)/shard_map/while/body/eval_jaxpr/ppermute | solution.py:25
  339.7 5.6 collective-permute-start
  351.4 17.9 %collective-permute-start.2 = (f32[4,8,8,512]{3,2,1,0:T(8,128)}, f32[4,8,8,512]{3,2,1,0:T(8,128)S(1)}, u32[]{:S(2)}, u32[]{:S(2)}) collective-permute-start(f32[4,8,8,512]{3,2,1,0:T(8,128)} %fusion.140), channel_id=1, source_target_pairs={{0,32},{32,64},{64,96},{96,128},{128,160},{160,192},{192,224},{224... | collective-permute-start | bytes 1572872 | tf_op jit(solution)/shard_map/while/body/eval_jaxpr/ppermute | solution.py:25
  371.5 5.6 collective-permute-start
  383.3 17.6 %collective-permute-start.2 = (f32[4,8,8,512]{3,2,1,0:T(8,128)}, f32[4,8,8,512]{3,2,1,0:T(8,128)S(1)}, u32[]{:S(2)}, u32[]{:S(2)}) collective-permute-start(f32[4,8,8,512]{3,2,1,0:T(8,128)} %fusion.140), channel_id=1, source_target_pairs={{0,32},{32,64},{64,96},{96,128},{128,160},{160,192},{192,224},{224... | collective-permute-start | bytes 1572872 | tf_op jit(solution)/shard_map/while/body/eval_jaxpr/ppermute | solution.py:25
  403.1 5.6 collective-permute-start
  414.8 17.3 %collective-permute-start.2 = (f32[4,8,8,512]{3,2,1,0:T(8,128)}, f32[4,8,8,512]{3,2,1,0:T(8,128)S(1)}, u32[]{:S(2)}, u32[]{:S(2)}) collective-permute-start(f32[4,8,8,512]{3,2,1,0:T(8,128)} %fusion.140), channel_id=1, source_target_pairs={{0,32},{32,64},{64,96},{96,128},{128,160},{160,192},{192,224},{224... | collective-permute-start | bytes 1572872 | tf_op jit(solution)/shard_map/while/body/eval_jaxpr/ppermute | solution.py:25
  434.3 5.6 collective-permute-start
  446.0 16.9 %collective-permute-start.2 = (f32[4,8,8,512]{3,2,1,0:T(8,128)}, f32[4,8,8,512]{3,2,1,0:T(8,128)S(1)}, u32[]{:S(2)}, u32[]{:S(2)}) collective-permute-start(f32[4,8,8,512]{3,2,1,0:T(8,128)} %fusion.140), channel_id=1, source_target_pairs={{0,32},{32,64},{64,96},{96,128},{128,160},{160,192},{192,224},{224... | collective-permute-start | bytes 1572872 | tf_op jit(solution)/shard_map/while/body/eval_jaxpr/ppermute | solution.py:25
  465.1 5.6 collective-permute-start
  476.9 16.6 %collective-permute-start.2 = (f32[4,8,8,512]{3,2,1,0:T(8,128)}, f32[4,8,8,512]{3,2,1,0:T(8,128)S(1)}, u32[]{:S(2)}, u32[]{:S(2)}) collective-permute-start(f32[4,8,8,512]{3,2,1,0:T(8,128)} %fusion.140), channel_id=1, source_target_pairs={{0,32},{32,64},{64,96},{96,128},{128,160},{160,192},{192,224},{224... | collective-permute-start | bytes 1572872 | tf_op jit(solution)/shard_map/while/body/eval_jaxpr/ppermute | solution.py:25
  495.6 5.6 collective-permute-start
  507.4 17.0 %collective-permute-start.2 = (f32[4,8,8,512]{3,2,1,0:T(8,128)}, f32[4,8,8,512]{3,2,1,0:T(8,128)S(1)}, u32[]{:S(2)}, u32[]{:S(2)}) collective-permute-start(f32[4,8,8,512]{3,2,1,0:T(8,128)} %fusion.140), channel_id=1, source_target_pairs={{0,32},{32,64},{64,96},{96,128},{128,160},{160,192},{192,224},{224... | collective-permute-start | bytes 1572872 | tf_op jit(solution)/shard_map/while/body/eval_jaxpr/ppermute | solution.py:25
  526.6 5.6 collective-permute-start
  538.4 17.3 %collective-permute-start.2 = (f32[4,8,8,512]{3,2,1,0:T(8,128)}, f32[4,8,8,512]{3,2,1,0:T(8,128)S(1)}, u32[]{:S(2)}, u32[]{:S(2)}) collective-permute-start(f32[4,8,8,512]{3,2,1,0:T(8,128)} %fusion.140), channel_id=1, source_target_pairs={{0,32},{32,64},{64,96},{96,128},{128,160},{160,192},{192,224},{224... | collective-permute-start | bytes 1572872 | tf_op jit(solution)/shard_map/while/body/eval_jaxpr/ppermute | solution.py:25
  557.8 5.6 collective-permute-start
  569.6 16.9 %collective-permute-start.2 = (f32[4,8,8,512]{3,2,1,0:T(8,128)}, f32[4,8,8,512]{3,2,1,0:T(8,128)S(1)}, u32[]{:S(2)}, u32[]{:S(2)}) collective-permute-start(f32[4,8,8,512]{3,2,1,0:T(8,128)} %fusion.140), channel_id=1, source_target_pairs={{0,32},{32,64},{64,96},{96,128},{128,160},{160,192},{192,224},{224... | collective-permute-start | bytes 1572872 | tf_op jit(solution)/shard_map/while/body/eval_jaxpr/ppermute | solution.py:25
  586.7 5.4 collective-permute-start.19
  588.7 5.7 collective-permute-start.18
  (182 other events, 1893.9 us)
where the time goes:
time: 613 us; the launch traced here: 601 us
  waiting for transfers between devices  279 us (46%)
  starting transfers between devices  164 us (27%)
  other arithmetic  124 us (20%)
  local copies, waits for them, and re-layouts  29.2 us (5%)
    ppermute x16, waiting for transfers between devices, from_behind(): return lax.ppermute(block, axis, route)  235 us
    ppermute x23, starting transfers between devices, with_halo(): lax.ppermute(lax.slice_in_dim(block, block.shape[dim] - width, None, axis...  70.6 us
    ppermute x23, starting transfers between devices, with_halo(): lax.ppermute(lax.slice_in_dim(block, 0, width, axis=dim), axis, backward)  58.8 us
    ppermute x23, waiting for transfers between devices, with_halo(): lax.ppermute(lax.slice_in_dim(block, block.shape[dim] - width, None, axis...  35.3 us
    add x15, other arithmetic, advance(): proposal = coarse_of(current, zero_offset, whole_width) + difference  34.5 us
    ppermute x16, starting transfers between devices, from_behind(): return lax.ppermute(block, axis, route)  34.3 us
    add x17, other arithmetic, coarse_step(): jnp.maximum(east_faces, 0.0) * padded[:, :, 0:cells_x + 1, 1:cells_y + 1]  25.5 us
    concatenate x16, local copies, waits for them, and re-layouts, with_halo(): block = jnp.concatenate([low, block, high], axis=dim)  20.9 us
  transfers between devices with their start and end apart: 62, of which 37 were waited for; matrix products, arithmetic and copies ran while one was open for 4% of the time, Pallas kernels for 0%

commit v1 on v0

v1 whole, which is shorter than its diff:
```python
import functools

import jax
import jax.numpy as jnp
from jax import lax
from jax.experimental import pallas as pl
from jax.experimental.pallas import tpu as pltpu
from jax.sharding import Mesh, PartitionSpec as P

TR, LEV, X, Y = 4, 8, 8, 512
SUB = 6
SLABS = 16
CHIPS = 16
LANE = 128
PIECES = Y // LANE
REACH = 12
ROWS = 2 * X
EXT = ROWS + 2 * REACH
CHUNK = 40
STATE = 8 * REACH
WIDE = jnp.float32
AXES = ("slab", "z", "core")


def split(value):
    return [value[:, LANE * k : LANE * (k + 1)] for k in range(PIECES)]


def join(parts):
    return jnp.concatenate(parts, axis=1)


def lane(k):
    return slice(LANE * k, LANE * (k + 1))


def from_right(parts):
    turned = [pltpu.roll(part, LANE - 1, 1) for part in parts] + [0.0]
    ends = lax.broadcasted_iota(jnp.int32, (8, LANE), 1) == LANE - 1
    return [jnp.where(ends, turned[k + 1], turned[k]) for k in range(PIECES)]


def from_left(parts):
    turned = [pltpu.roll(part, 1, 1) for part in parts] + [0.0]
    ends = lax.broadcasted_iota(jnp.int32, (8, LANE), 1) == 0
    return [jnp.where(ends, turned[k - 1], turned[k]) for k in range(PIECES)]


def minmod(a, b):
    return jnp.maximum(jnp.minimum(a, b), jnp.minimum(jnp.maximum(a, b), 0.0))


def each(function, *lists):
    return [function(*items) for items in zip(*lists)]


def minus(a, b):
    return each(lambda p, q: p - q, a, b)


def call(kernel, shapes, in_specs, scratch=(), flops=1000000, nbytes=1000000, vmem=24 << 20):
    whole = pl.BlockSpec(memory_space=pltpu.VMEM)
    spaces = {
        "v": whole,
        "s": pl.BlockSpec(memory_space=pltpu.SMEM),
        "h": pl.BlockSpec(memory_space=pl.ANY),
    }
    return pl.pallas_call(
        kernel,
        out_shape=[jax.ShapeDtypeStruct(shape, WIDE) for shape in shapes],
        in_specs=[spaces[kind] for kind in in_specs],
        out_specs=[whole] * len(shapes),
        scratch_shapes=list(scratch),
        compiler_params=pltpu.CompilerParams(vmem_limit_bytes=vmem),
        cost_estimate=pl.CostEstimate(flops=flops, bytes_accessed=nbytes, transcendentals=0),
    )


def to_tiles(array):
    rows = array.shape[0] // 8
    return array.reshape(rows, 8, PIECES, LANE).transpose(0, 2, 1, 3)


def from_tiles(array):
    rows = array.shape[0] // (8 * PIECES)
    return array.reshape(rows, PIECES, 8, LANE).transpose(0, 2, 1, 3).reshape(-1, Y)


def prepare_kernel(count, s_ref, e_ref, n_ref, k_ref, out, held, sems):
    slab = lax.axis_index("slab")
    copies = [pltpu.make_async_copy(s_ref, out.at[:, pl.ds(0, 32), :], sems.at[0])]
    for q, ref in enumerate((e_ref, n_ref, k_ref)):
        copies.append(
            pltpu.make_async_copy(ref, held.at[:, pl.ds(32 * q, 32), :], sems.at[q + 1])
        )
    for copy in copies:
        copy.start()
    for copy in copies[1:]:
        copy.wait()
    number = jnp.full((8, LANE), count[0, 0].astype(WIDE), WIDE)
    row = lax.broadcasted_iota(jnp.int32, (8, LANE), 0)
    held[:, 96:104, :] = jnp.zeros((LEV, 8, LANE), WIDE)
    for level in range(LEV):
        part = held[level, pl.ds(6 * slab, 8), :]
        part = jnp.where(row < 6, part, number)
        for tracer in range(TR):
            out[tracer * LEV + level, 32:40, :] = part
    copies[0].wait()


def state_row(arrived, half, row, k):
    start = (2 * 8 * half + row // 8) * CHUNK + 8 * k + row % 8
    return arrived[pl.ds(start, 8, stride=2 * CHUNK), :]


def arrange_kernel(half, arrived, *refs):
    to_next, to_prev = refs[-2:]
    for i in range(REACH):
        for k in range(PIECES):
            to_next[8 * i : 8 * i + 8, lane(k)] = state_row(arrived, half, i + 4, k)
            to_prev[8 * i : 8 * i + 8, lane(k)] = state_row(arrived, half, i, k)
    if half:
        return
    for n in range(SLABS):
        for core in range(2):
            base = (2 * n + core) * CHUNK + 32
            j = 6 * n
            while j < 6 * n + 6:
                stop = min(6 * n + 6, j // 8 * 8 + 8)
                q, k, x = j // 32, j % 32 // 8, j % 8
                piece = arrived[base + j - 6 * n : base + stop - 6 * n, :]
                at = STATE + 16 * q + 8 * core + x
                to_next[at : at + stop - j, lane(k)] = piece
                to_prev[at : at + stop - j, lane(k)] = piece
                j = stop
    for core in range(2):
        for group in range(2):
            start = (16 * group + core) * CHUNK + 38
            piece = arrived[pl.ds(start, 8, stride=2 * CHUNK), :]
            at = STATE + 48
            to_next[at : at + 8, lane(2 * group + core)] = piece
            to_prev[at : at + 8, lane(2 * group + core)] = piece


def next_offset(n):
    return 8 + sum(15 - m for m in range(n // 8 * 8, n))


def prev_offset(n):
    return sum(15 - m for m in range(n + 1, n // 8 * 8 + 8))


def fine_kernel(half, arrived, mine, low_head, high_head, low, high, *refs):
    out, to_next, to_prev, field, wx, kk, ax, axw, py, my, pq, mq, steps, frac = refs[-14:]

    def edge_state(i, carry):
        at = pl.ds(pl.multiple_of(8 * i, 8), 8)
        field[0, i + 2] = low[at, :]
        field[0, i + 2 + REACH + ROWS] = high[at, :]
        return carry

    lax.fori_loop(0, REACH, edge_state, 0)

    def own_state(r, carry):
        for k in range(PIECES):
            field[0, r + 2 + REACH, :, lane(k)] = state_row(arrived, half, r, k)
        return carry

    lax.fori_loop(0, ROWS, own_state, 0)
    for tile in range(6):
        ref = (low_head, mine, high_head)[tile // 2]
        at = STATE + 48
        number = ref[at : at + 8, lane(2 * half + tile % 2)]
        steps[tile] = number
        frac[tile] = 1.0 / jnp.maximum(number, 1.0)

    def spread_rows(ref, first, shift):
        def one(i, carry):
            for q, target in enumerate((wx, py, kk)):
                row = ref[pl.ds(STATE + 16 * q + first + i, 1), :]
                target[i + first + shift] = jnp.broadcast_to(row, (8, Y))
            return carry

        return one

    lax.fori_loop(0, REACH, spread_rows(low_head, ROWS - REACH, REACH + 2 - ROWS), 0)
    lax.fori_loop(0, ROWS, spread_rows(mine, 0, REACH + 2), 0)
    lax.fori_loop(0, REACH, spread_rows(high_head, 0, REACH + ROWS + 2), 0)

    def limited(size, half_fraction):
        return size * (0.5 - half_fraction * size)

    def coefficients(i, carry):
        r = 4 * i + 2
        part = 0.5 * frac[(r + 2) // 8]
        half_fraction = join([part] * PIECES)
        axw[i] = limited(jnp.abs(wx[r - 1]), half_fraction)
        for j in range(4):
            ax[r + j] = limited(jnp.abs(wx[r + j]), half_fraction)
            north = py[r + j]
            south = join(from_left(split(north)))
            forward, backward = jnp.maximum(north, 0.0), jnp.minimum(south, 0.0)
            py[r + j] = forward
            my[r + j] = backward
            pq[r + j] = limited(forward, half_fraction)
            mq[r + j] = limited(-backward, half_fraction)
        return carry

    lax.fori_loop(0, EXT // 4, coefficients, 0)

    def flux(w, a, here, there, slope_here, slope_there):
        up = w > 0.0
        return w * jnp.where(up, here, there) + a * jnp.where(up, slope_here, slope_there)

    def outgoing(a, b, value, slope):
        return a * value + b * slope

    def block(substep, source, target, index):
        r = 4 * index + 2
        tile = (r + 2) // 8
        f = jnp.where(steps[tile] > substep.astype(WIDE), frac[tile], 0.0)
        c = {i: split(field[source, r + i]) for i in range(-2, 6)}
        dx = {i: minus(c[i + 1], c[i]) for i in range(-2, 5)}
        sx = {i: each(minmod, dx[i], dx[i - 1]) for i in range(-1, 5)}
        fx = {}
        for i in range(-1, 4):
            a = split(ax[r + i] if i >= 0 else axw[index])
            fx[i] = each(flux, split(wx[r + i]), a, c[i], c[i + 1], sx[i], sx[i + 1])
        for i in range(4):
            dy = minus(from_right(c[i]), c[i])
            dy_left = minus(c[i], from_left(c[i]))
            sy = each(minmod, dy, dy_left)
            north = each(outgoing, split(py[r + i]), split(pq[r + i]), c[i], sy)
            south = each(outgoing, split(my[r + i]), split(mq[r + i]), c[i], sy)
            north_left = from_left(north)
            south_right = from_right(south)
            k_row = split(kk[r + i])
            for p in range(PIECES):
                spread = (dx[i][p] - dx[i - 1][p]) + (dy[p] - dy_left[p])
                along = (north_left[p] - north[p]) + (south[p] - south_right[p])
                rate = (fx[i - 1][p] - fx[i][p]) + along + k_row[p] * spread
                field[target, r + i, :, lane(p)] = c[i][p] + f * rate

    def substep_blocks(substep, carry):
        source = jnp.where(substep == 0, 0, 1 + (substep + 1) % 2)
        target = 1 + substep % 2
        first = (substep + 1) // 2
        lax.fori_loop(
            first,
            EXT // 4 - first,
            lambda index, _: block(substep, source, target, index),
            None,
        )
        return carry

    lax.fori_loop(0, SUB, substep_blocks, 0)
    final = 1 + (SUB - 1) % 2
    if half == 0:
        later = jnp.where(lax.broadcasted_iota(jnp.int32, (8, LANE), 0) > 0, 1.0, 0.0)
    else:
        later = jnp.ones((8, LANE), WIDE)

    def upwind(w, here, there):
        return w * jnp.where(w > 0.0, here, there)

    def compare(index, carry):
        r = 2 * index + REACH + 2
        c = {j: split(field[0, r + j]) for j in range(-1, 3)}
        fx = [each(upwind, split(wx[r + j]), c[j], c[j + 1]) for j in (-1, 0, 1)]
        for j in range(2):
            right = from_right(c[j])
            left = from_left(c[j])
            north = each(lambda a, b: a * b, split(py[r + j]), c[j])
            south = each(lambda a, b: a * b, split(my[r + j]), c[j])
            north_left = from_left(north)
            south_right = from_right(south)
            end = split(field[final, r + j])
            k_row = split(kk[r + j])
            i = 2 * index + j
            for p in range(PIECES):
                spread = c[j - 1][p] + c[j + 1][p] + left[p] + right[p] - 4.0 * c[j][p]
                along = (north_left[p] - north[p]) + (south[p] - south_right[p])
                coarse = c[j][p] + (fx[j][p] - fx[j + 1][p]) + along + k_row[p] * spread
                at = (i // 8) * 32 + 8 * p + i % 8
                out[pl.ds(at, 8, stride=64), :] = end[p] - later * coarse
        return carry

    lax.fori_loop(0, ROWS // 2, compare, 0)

    to_next[0:8, :] = jnp.zeros((8, Y), WIDE)
    used = next_offset(8 * half + 7) + 8 - 8 * half
    for ref, filled in ((to_next, used), (to_prev, used - 8)):
        total = ref.shape[0]
        ref[filled:total, :] = jnp.zeros((total - filled, Y), WIDE)
    for n in range(8 * half, min(8 * half + 8, 15)):
        rows = 15 - n
        for k in range(PIECES):

            def piece(first, last, upper):
                at = (2 * (n - 8 * half) + upper) * 32 + 8 * k
                return out[at + first : at + last, :]

            at = next_offset(n)
            if rows > 8:
                to_next[at : at + rows - 8, lane(k)] = piece(16 - rows, 8, 0)
                to_next[at + rows - 8 : at + rows, lane(k)] = piece(0, 8, 1)
            else:
                to_next[at : at + rows, lane(k)] = piece(8 - rows, 8, 1)
            at = prev_offset(n)
            if rows > 8:
                to_prev[at : at + 8, lane(k)] = piece(0, 8, 0)
                to_prev[at + 8 : at + rows, lane(k)] = piece(0, rows - 8, 1)
            else:
                to_prev[at : at + rows, lane(k)] = piece(0, rows, 0)


def from_below(tiles):
    row = lax.broadcasted_iota(jnp.int32, (8, LANE), 0)
    turned = [[pltpu.roll(part, 1, 0) for part in tile] for tile in tiles]
    return [
        [jnp.where(row == 0, turned[max(k - 1, 0)][p], turned[k][p]) for p in range(PIECES)]
        for k in range(len(tiles))
    ]


def from_above(tiles):
    row = lax.broadcasted_iota(jnp.int32, (8, LANE), 0)
    turned = [[pltpu.roll(part, 7, 0) for part in tile] for tile in tiles]
    top = len(tiles) - 1
    return [
        [jnp.where(row == 7, turned[min(k + 1, top)][p], turned[k][p]) for p in range(PIECES)]
        for k in range(len(tiles))
    ]


def rows_at(ref, at):
    return split(ref[at : at + 8, :])


def differences(half, n, own, low, high):
    size = 8 if half else 16
    tiles = []
    if n < 15:
        at = next_offset(n) + 15 - n - size
        tiles += [rows_at(low, at + 8 * k) for k in range(size // 8)]
    at = 16 * (n - 8 * half)
    tiles += [rows_at(own, at), rows_at(own, at + 8)]
    if n < 15:
        at = prev_offset(n)
        tiles += [rows_at(high, at + 8 * k) for k in range(size // 8)]
    return tiles


def advance(value, first, added, stencil, inside, keep=None):
    above, below = from_above(value), from_below(value)
    if keep:
        value, above, below = value[keep], above[keep], below[keep]
        first += keep.start
    result = []
    for k in range(len(value)):
        right, left = from_right(value[k]), from_left(value[k])
        parts = []
        for p in range(PIECES):
            a = [stencil[j, pl.ds(8 * (k + first), 8), lane(p)] for j in range(5)]
            moved = (
                (a[0] * value[k][p] + added[k][p])
                + (a[1] * above[k][p] + a[2] * below[k][p])
                + (a[3] * right[p] + a[4] * left[p])
            )
            parts.append(moved * inside if k + first >= 4 else moved)
        result.append(parts)
    return result


def first_chain_kernel(own, mine, low_head, high_head, low, high, out, stencil, state):
    inside = jnp.where(lax.axis_index("z") < CHIPS - 1, 1.0, 0.0).astype(WIDE)

    def rows_of(q):
        return [
            rows_at(ref, STATE + 16 * q + 8 * upper)
            for ref in (low_head, mine, high_head)
            for upper in range(2)
        ]

    east, north, spread = rows_of(0), rows_of(1), rows_of(2)
    west = from_below(east)
    for k in range(6):
        south = from_left(north[k])
        for p in range(PIECES):
            at = (pl.ds(8 * k, 8), lane(p))
            e, w, n, s, d = east[k][p], west[k][p], north[k][p], south[p], spread[k][p]
            outward = jnp.maximum(e, 0.0) - jnp.minimum(w, 0.0)
            outward = outward + (jnp.maximum(n, 0.0) - jnp.minimum(s, 0.0))
            stencil[0, at[0], at[1]] = 1.0 - outward - 4.0 * d
            stencil[1, at[0], at[1]] = d - jnp.minimum(e, 0.0)
            stencil[2, at[0], at[1]] = d + jnp.maximum(w, 0.0)
            stencil[3, at[0], at[1]] = d - jnp.minimum(n, 0.0)
            stencil[4, at[0], at[1]] = d + jnp.maximum(s, 0.0)

    value = differences(0, 0, own, low, high)
    for n in range(8):
        if n:
            value = advance(value, 0, differences(0, n, own, low, high), stencil, inside)
        for k in range(2):
            out[16 * n + 8 * k : 16 * n + 8 * k + 8, :] = join(value[k + 2])
    for k in range(4):
        state[8 * k : 8 * k + 8, :] = join(value[k + 1])


def second_chain_kernel(own, low, high, done, stencil, state, out):
    inside = jnp.where(lax.axis_index("z") < CHIPS - 1, 1.0, 0.0).astype(WIDE)
    out[0:128, :] = done[...]
    value = [rows_at(state, 8 * k) for k in range(4)]
    for n in range(8, 16):
        added = differences(1, n, own, low, high)
        keep = slice(1, 3) if n == 15 else None
        value = advance(value, 1, added, stencil, inside, keep)
        for k in range(2):
            at = 16 * n + 8 * k
            out[at : at + 8, :] = join(value[k if keep else k + 1])


def device_at(slab, z, core):
    return (slab * CHIPS + z) * 2 + core


def to_chip(array, step):
    route = [
        (device_at(p, z, c), device_at(p, z + step, c))
        for p in range(SLABS)
        for z in range(CHIPS)
        for c in range(2)
        if 0 <= z + step < CHIPS
    ]
    return lax.ppermute(array, AXES, route)


def on_device(slab_starts, substeps, east_velocity, north_velocity, diffusivity):
    fields = to_tiles(slab_starts.reshape(TR * LEV * X, Y)).reshape(TR * LEV, 32, LANE)
    speeds = [
        to_tiles(a.reshape(LEV * X, Y)).reshape(LEV, 32, LANE)
        for a in (east_velocity, north_velocity, diffusivity)
    ]
    (sent,) = call(
        prepare_kernel,
        [(TR * LEV, CHUNK, LANE)],
        "shhhh",
        scratch=[pltpu.VMEM((LEV, 104, LANE), WIDE), pltpu.SemaphoreType.DMA((4,))],
        flops=300000,
        nbytes=2000000,
        vmem=63 << 20,
    )(substeps, fields, *speeds)
    arrived = lax.all_to_all(sent, ("slab", "core"), 0, 0, tiled=True)
    arrived = arrived.reshape(TR * LEV * CHUNK, LANE)

    head = STATE + 56
    next_a, prev_a = call(functools.partial(arrange_kernel, 0), [(head, Y), (head, Y)], "v")(
        arrived
    )
    low_a, high_a = to_chip(next_a, 1), to_chip(prev_a, -1)
    next_b, prev_b = call(
        functools.partial(arrange_kernel, 1), [(STATE, Y), (STATE, Y)], "vh"
    )(arrived, next_a)
    low_b, high_b = to_chip(next_b, 1), to_chip(prev_b, -1)

    rows = pltpu.VMEM((EXT + 4, 8, Y), WIDE)
    scratch = [
        pltpu.VMEM((3, EXT + 4, 8, Y), WIDE),
        rows,
        rows,
        rows,
        pltpu.VMEM((EXT // 4, 8, Y), WIDE),
        rows,
        rows,
        rows,
        rows,
        pltpu.VMEM((6, 8, LANE), WIDE),
        pltpu.VMEM((6, 8, LANE), WIDE),
    ]
    own_a, next_c, prev_c = call(
        functools.partial(fine_kernel, 0),
        [(512, LANE), (104, Y), (104, Y)],
        "vvvvvv",
        scratch=scratch,
        flops=25000000,
        nbytes=3000000,
    )(arrived, next_a, low_a, high_a, low_a, high_a)
    low_c, high_c = to_chip(next_c, 1), to_chip(prev_c, -1)
    own_b, next_d, prev_d = call(
        functools.partial(fine_kernel, 1),
        [(512, LANE), (40, Y), (40, Y)],
        "vvvvvvh",
        scratch=scratch,
        flops=25000000,
        nbytes=3000000,
    )(arrived, next_a, low_a, high_a, low_b, high_b, next_c)
    low_d, high_d = to_chip(next_d, 1), to_chip(prev_d, -1)
    own_a, own_b = [from_tiles(a) for a in (own_a, own_b)]
    done, stencil, state = call(
        first_chain_kernel, [(128, Y), (5, 48, Y), (32, Y)], "vvvvvv", flops=5000000
    )(own_a, next_a, low_a, high_a, low_c, high_c)
    (chain,) = call(second_chain_kernel, [(256, Y)], "vvvvvv", flops=3000000)(
        own_b, low_d, high_d, done, stencil, state
    )
    result = lax.all_to_all(
        chain.reshape(SLABS * 2, 8, Y), ("slab", "core"), 0, 0, tiled=True
    )
    return result.reshape(1, TR, LEV, X, Y)


def solution(mesh):
    fine_mesh = Mesh(mesh.devices.reshape(SLABS, CHIPS, 2), AXES)
    tile = ("z", "core")
    return jax.shard_map(
        on_device,
        mesh=fine_mesh,
        in_specs=(
            P("slab", None, None, tile, None),
            P("slab", tile),
            P(None, tile, None),
            P(None, tile, None),
            P(None, tile, None),
        ),
        out_specs=P("slab", None, None, tile, None),
        check_vma=False,
    )
```

time: 613 us -> 95.9 us (0.16)
  the two profiles are of different devices: /device:TPU:194 before, /device:TPU:97 now
where the time goes in v1:
time: 95.9 us; the launch traced here: 95.4 us
  blocking collectives  39.1 us (41%)
  Pallas kernels  24.9 us (26%)
  starting transfers between devices  24.7 us (26%)
  waiting for transfers between devices  5.1 us (5%)
    ppermute x8, starting transfers between devices, to_chip(): return lax.ppermute(array, AXES, route)  24.7 us
    all_to_all x1, blocking collectives, on_device(): arrived = lax.all_to_all(sent, ('slab', 'core'), 0, 0, tiled=True)  20.7 us
    all_to_all x1, blocking collectives, on_device(): lax.all_to_all(chain.reshape(SLABS * 2, 8, Y), ('slab', 'core'), 0, 0, ti...  18.4 us
    pallas_call x1, Pallas kernels, on_device(): call(functools.partial(fine_kernel, 0), [(512, LANE), (104, Y), (104, Y)]...  10.7 us
    pallas_call x1, Pallas kernels, on_device(): call(functools.partial(fine_kernel, 1), [(512, LANE), (40, Y), (40, Y)],...  10.7 us
    ppermute x8, waiting for transfers between devices, to_chip(): return lax.ppermute(array, AXES, route)  5.1 us
    pallas_call x1, Pallas kernels, on_device(): call(prepare_kernel, [(TR * LEV, CHUNK, LANE)], 'shhhh', scratch=[pltpu.V...  2.03 us
  transfers between devices with their start and end apart: 8, of which 3 were waited for; matrix products, arithmetic and copies ran while one was open for 0% of the time, Pallas kernels for 23%

profile of v1, /device:TPU:97, one launch (start us, length us, event | category | flops | bytes accessed | tf_op | source)
XLA Modules:
  0.0 95.4 jit_solution(6901368254115494731)
XLA Ops:
  0.7 2.0 %shard_map.55 = f32[32,40,128]{2,1,0:T(8,128)} custom-call(s32[1,1]{1,0:T(1,128)S(6)} %copy.7.count, f32[32,32,128]{2,1,0:T(8,128)} %bitcast.41, f32[8,32,128]{2,1,0:T(8,128)} %bitcast.42, f32[8,32,128]{2,1,0:T(8,128)} %bitcast.43, f32[8,32,128]{2,1,0:T(8,128)} %bitcast.44), custom_call_target="tpu_custom_call" | custom-call | flops 300000 | bytes 2000000 | tf_op jit(solution)/shard_map/pallas_call | solution.py:444
  2.7 20.7 %all_to_all.10 = f32[32,40,128]{2,1,0:T(8,128)S(1)} all-to-all(f32[32,40,128]{2,1,0:T(8,128)} %shard_map.55), channel_id=1, replica_groups=mesh['slab'=16,'z'=16,'core'=2] {'slab','core'}, dimensions={0} | all-to-all | bytes 1310720 | tf_op jit(solution)/shard_map/all_to_all | solution.py:453
  23.4 0.1 shard_map.56
  23.5 1.9 %collective-permute-start.1 = (f32[152,512]{1,0:T(8,128)S(1)}, f32[152,512]{1,0:T(8,128)S(1)}, u32[]{:S(2)}, u32[]{:S(2)}) collective-permute-start(f32[152,512]{1,0:T(8,128)S(1)} %get-tuple-element.19), channel_id=1, source_target_pairs={{2,0},{3,1},{4,2},{5,3},{6,4},{7,5},{8,6},{9,7},{10,8},{11,9},{12,... | collective-permute-start | bytes 933896 | tf_op jit(solution)/shard_map/ppermute | solution.py:435
  25.4 4.8 %collective-permute-start = (f32[152,512]{1,0:T(8,128)S(1)}, f32[152,512]{1,0:T(8,128)S(1)}, u32[]{:S(2)}, u32[]{:S(2)}) collective-permute-start(f32[152,512]{1,0:T(8,128)S(1)} %get-tuple-element.18.refs_0_.mine), channel_id=1, source_target_pairs={{0,2},{1,3},{2,4},{3,5},{4,6},{5,7},{6,8},{7,9},{8,10},{9,11},{10,... | collective-permute-start | bytes 933896 | tf_op jit(solution)/shard_map/ppermute | solution.py:435
  30.2 0.1 shard_map.57
  30.3 3.5 %collective-permute-start.2 = (f32[96,512]{1,0:T(8,128)S(1)}, f32[96,512]{1,0:T(8,128)S(1)}, u32[]{:S(2)}, u32[]{:S(2)}) collective-permute-start(f32[96,512]{1,0:T(8,128)S(1)} %get-tuple-element.20), channel_id=1, source_target_pairs={{0,2},{1,3},{2,4},{3,5},{4,6},{5,7},{6,8},{7,9},{8,10},{9,11},{10,... | collective-permute-start | bytes 589832 | tf_op jit(solution)/shard_map/ppermute | solution.py:435
  33.9 1.9 %collective-permute-start.3 = (f32[96,512]{1,0:T(8,128)S(1)}, f32[96,512]{1,0:T(8,128)S(1)}, u32[]{:S(2)}, u32[]{:S(2)}) collective-permute-start(f32[96,512]{1,0:T(8,128)S(1)} %get-tuple-element.21), channel_id=1, source_target_pairs={{2,0},{3,1},{4,2},{5,3},{6,4},{7,5},{8,6},{9,7},{10,8},{11,9},{12,... | collective-permute-start | bytes 589832 | tf_op jit(solution)/shard_map/ppermute | solution.py:435
  35.8 0.3 collective-permute-done.1.high_head.high
  36.1 1.0 %collective-permute-done.low_head.low = f32[152,512]{1,0:T(8,128)S(1)} collective-permute-done((f32[152,512]{1,0:T(8,128)S(1)}, f32[152,512]{1,0:T(8,128)S(1)}, u32[]{:S(2)}, u32[]{:S(2)}) %collective-permute-start) | collective-permute-done | bytes 311328 | tf_op jit(solution)/shard_map/ppermute | solution.py:435
  37.1 10.7 %shard_map.58 = (f32[512,128]{1,0:T(8,128)S(1)}, f32[104,512]{1,0:T(8,128)S(1)}, f32[104,512]{1,0:T(8,128)S(1)}) custom-call(f32[1280,128]{1,0:T(8,128)S(1)} %bitcast.35, f32[152,512]{1,0:T(8,128)S(1)} %get-tuple-element.18.refs_0_.mine, f32[152,512]{1,0:T(8,128)S(1)} %collective-permute-done.low_head.low, ...), custom_call_target="tpu_custom_call" | custom-call | flops 25000000 | bytes 3000000 | tf_op jit(solution)/shard_map/pallas_call | solution.py:480
  47.8 1.9 %collective-permute-start.7 = (f32[104,512]{1,0:T(8,128)S(1)}, f32[104,512]{1,0:T(8,128)S(1)}, u32[]{:S(2)}, u32[]{:S(2)}) collective-permute-start(f32[104,512]{1,0:T(8,128)S(1)} %get-tuple-element.27), channel_id=1, source_target_pairs={{2,0},{3,1},{4,2},{5,3},{6,4},{7,5},{8,6},{9,7},{10,8},{11,9},{12,... | collective-permute-start | bytes 638984 | tf_op jit(solution)/shard_map/ppermute | solution.py:435
  49.7 5.3 %collective-permute-start.6 = (f32[104,512]{1,0:T(8,128)S(1)}, f32[104,512]{1,0:T(8,128)S(1)}, u32[]{:S(2)}, u32[]{:S(2)}) collective-permute-start(f32[104,512]{1,0:T(8,128)S(1)} %get-tuple-element.22.refs_0_), channel_id=1, source_target_pairs={{0,2},{1,3},{2,4},{3,5},{4,6},{5,7},{6,8},{7,9},{8,10},{9,11},{10,... | collective-permute-start | bytes 638984 | tf_op jit(solution)/shard_map/ppermute | solution.py:435
  55.1 0.0 collective-permute-done.2.low
  55.1 0.0 collective-permute-done.3.high
  55.1 10.7 %shard_map.59 = (f32[512,128]{1,0:T(8,128)S(1)}, f32[40,512]{1,0:T(8,128)S(1)}, f32[40,512]{1,0:T(8,128)S(1)}) custom-call(f32[1280,128]{1,0:T(8,128)S(1)} %bitcast.36, f32[152,512]{1,0:T(8,128)S(1)} %get-tuple-element.18.refs_0_.mine, f32[152,512]{1,0:T(8,128)S(1)} %collective-permute-done.low_head.low, ...), custom_call_target="tpu_custom_call" | custom-call | flops 25000000 | bytes 3000000 | tf_op jit(solution)/shard_map/pallas_call | solution.py:489
  65.8 3.4 %collective-permute-start.4 = (f32[40,512]{1,0:T(8,128)S(1)}, f32[40,512]{1,0:T(8,128)S(1)}, u32[]{:S(2)}, u32[]{:S(2)}) collective-permute-start(f32[40,512]{1,0:T(8,128)S(1)} %get-tuple-element.24), channel_id=1, source_target_pairs={{0,2},{1,3},{2,4},{3,5},{4,6},{5,7},{6,8},{7,9},{8,10},{9,11},{10,... | collective-permute-start | bytes 245768 | tf_op jit(solution)/shard_map/ppermute | solution.py:435
  69.2 1.9 %collective-permute-start.5 = (f32[40,512]{1,0:T(8,128)S(1)}, f32[40,512]{1,0:T(8,128)S(1)}, u32[]{:S(2)}, u32[]{:S(2)}) collective-permute-start(f32[40,512]{1,0:T(8,128)S(1)} %get-tuple-element.25), channel_id=1, source_target_pairs={{2,0},{3,1},{4,2},{5,3},{6,4},{7,5},{8,6},{9,7},{10,8},{11,9},{12,... | collective-permute-start | bytes 245768 | tf_op jit(solution)/shard_map/ppermute | solution.py:435
  71.1 0.0 collective-permute-done.7.high
  71.1 0.0 collective-permute-done.6.low
  71.1 0.6 shard_map.60
  71.8 0.0 collective-permute-done.4.low
  71.8 3.8 %collective-permute-done.5.high = f32[40,512]{1,0:T(8,128)S(1)} collective-permute-done((f32[40,512]{1,0:T(8,128)S(1)}, f32[40,512]{1,0:T(8,128)S(1)}, u32[]{:S(2)}, u32[]{:S(2)}) %collective-permute-start.5) | collective-permute-done | bytes 81952 | tf_op jit(solution)/shard_map/ppermute | solution.py:435
  75.6 0.6 shard_map.61
  76.2 18.4 %all_to_all.11 = f32[32,8,512]{2,1,0:T(8,128)S(1)} all-to-all(f32[32,8,512]{2,1,0:T(8,128)S(1)} %bitcast.37), channel_id=1, replica_groups=mesh['slab'=16,'z'=16,'core'=2] {'slab','core'}, dimensions={0} | all-to-all | bytes 1048576 | tf_op jit(solution)/shard_map/all_to_all | solution.py:505
  94.6 0.8 copy.8
Async XLA Ops:
  23.5 12.6 %collective-permute-start.1 = (f32[152,512]{1,0:T(8,128)S(1)}, f32[152,512]{1,0:T(8,128)S(1)}, u32[]{:S(2)}, u32[]{:S(2)}) collective-permute-start(f32[152,512]{1,0:T(8,128)S(1)} %get-tuple-element.19), channel_id=1, source_target_pairs={{2,0},{3,1},{4,2},{5,3},{6,4},{7,5},{8,6},{9,7},{10,8},{11,9},{12,... | collective-permute-start | bytes 933896 | tf_op jit(solution)/shard_map/ppermute | solution.py:435
  25.4 11.6 %collective-permute-start = (f32[152,512]{1,0:T(8,128)S(1)}, f32[152,512]{1,0:T(8,128)S(1)}, u32[]{:S(2)}, u32[]{:S(2)}) collective-permute-start(f32[152,512]{1,0:T(8,128)S(1)} %get-tuple-element.18.refs_0_.mine), channel_id=1, source_target_pairs={{0,2},{1,3},{2,4},{3,5},{4,6},{5,7},{6,8},{7,9},{8,10},{9,11},{10,... | collective-permute-start | bytes 933896 | tf_op jit(solution)/shard_map/ppermute | solution.py:435
  30.3 24.8 %collective-permute-start.2 = (f32[96,512]{1,0:T(8,128)S(1)}, f32[96,512]{1,0:T(8,128)S(1)}, u32[]{:S(2)}, u32[]{:S(2)}) collective-permute-start(f32[96,512]{1,0:T(8,128)S(1)} %get-tuple-element.20), channel_id=1, source_target_pairs={{0,2},{1,3},{2,4},{3,5},{4,6},{5,7},{6,8},{7,9},{8,10},{9,11},{10,... | collective-permute-start | bytes 589832 | tf_op jit(solution)/shard_map/ppermute | solution.py:435
  33.9 21.2 %collective-permute-start.3 = (f32[96,512]{1,0:T(8,128)S(1)}, f32[96,512]{1,0:T(8,128)S(1)}, u32[]{:S(2)}, u32[]{:S(2)}) collective-permute-start(f32[96,512]{1,0:T(8,128)S(1)} %get-tuple-element.21), channel_id=1, source_target_pairs={{2,0},{3,1},{4,2},{5,3},{6,4},{7,5},{8,6},{9,7},{10,8},{11,9},{12,... | collective-permute-start | bytes 589832 | tf_op jit(solution)/shard_map/ppermute | solution.py:435
  47.8 23.3 %collective-permute-start.7 = (f32[104,512]{1,0:T(8,128)S(1)}, f32[104,512]{1,0:T(8,128)S(1)}, u32[]{:S(2)}, u32[]{:S(2)}) collective-permute-start(f32[104,512]{1,0:T(8,128)S(1)} %get-tuple-element.27), channel_id=1, source_target_pairs={{2,0},{3,1},{4,2},{5,3},{6,4},{7,5},{8,6},{9,7},{10,8},{11,9},{12,... | collective-permute-start | bytes 638984 | tf_op jit(solution)/shard_map/ppermute | solution.py:435
  49.7 21.4 %collective-permute-start.6 = (f32[104,512]{1,0:T(8,128)S(1)}, f32[104,512]{1,0:T(8,128)S(1)}, u32[]{:S(2)}, u32[]{:S(2)}) collective-permute-start(f32[104,512]{1,0:T(8,128)S(1)} %get-tuple-element.22.refs_0_), channel_id=1, source_target_pairs={{0,2},{1,3},{2,4},{3,5},{4,6},{5,7},{6,8},{7,9},{8,10},{9,11},{10,... | collective-permute-start | bytes 638984 | tf_op jit(solution)/shard_map/ppermute | solution.py:435
  65.8 6.0 %collective-permute-start.4 = (f32[40,512]{1,0:T(8,128)S(1)}, f32[40,512]{1,0:T(8,128)S(1)}, u32[]{:S(2)}, u32[]{:S(2)}) collective-permute-start(f32[40,512]{1,0:T(8,128)S(1)} %get-tuple-element.24), channel_id=1, source_target_pairs={{0,2},{1,3},{2,4},{3,5},{4,6},{5,7},{6,8},{7,9},{8,10},{9,11},{10,... | collective-permute-start | bytes 245768 | tf_op jit(solution)/shard_map/ppermute | solution.py:435
  69.2 6.4 %collective-permute-start.5 = (f32[40,512]{1,0:T(8,128)S(1)}, f32[40,512]{1,0:T(8,128)S(1)}, u32[]{:S(2)}, u32[]{:S(2)}) collective-permute-start(f32[40,512]{1,0:T(8,128)S(1)} %get-tuple-element.25), channel_id=1, source_target_pairs={{2,0},{3,1},{4,2},{5,3},{6,4},{7,5},{8,6},{9,7},{10,8},{11,9},{12,... | collective-permute-start | bytes 245768 | tf_op jit(solution)/shard_map/ppermute | solution.py:435

commit v2 on v1

--- a/solution.py
+++ b/solution.py
@@ -86,18 +86,19 @@
     return array.reshape(rows, PIECES, 8, LANE).transpose(0, 2, 1, 3).reshape(-1, Y)
 
 
-def prepare_kernel(count, s_ref, e_ref, n_ref, k_ref, out, held, sems):
+def prepare_kernel(count_ref, s_ref, e_ref, n_ref, k_ref, out, held, count, sems):
     slab = lax.axis_index("slab")
     copies = [pltpu.make_async_copy(s_ref, out.at[:, pl.ds(0, 32), :], sems.at[0])]
     for q, ref in enumerate((e_ref, n_ref, k_ref)):
         copies.append(
             pltpu.make_async_copy(ref, held.at[:, pl.ds(32 * q, 32), :], sems.at[q + 1])
         )
+    copies.append(pltpu.make_async_copy(count_ref, count, sems.at[4]))
     for copy in copies:
         copy.start()
     for copy in copies[1:]:
         copy.wait()
-    number = jnp.full((8, LANE), count[0, 0].astype(WIDE), WIDE)
+    number = jnp.broadcast_to(count[...].astype(WIDE), (8, LANE))
     row = lax.broadcasted_iota(jnp.int32, (8, LANE), 0)
     held[:, 96:104, :] = jnp.zeros((LEV, 8, LANE), WIDE)
     for level in range(LEV):
@@ -151,19 +152,19 @@
 
 
 def fine_kernel(half, arrived, mine, low_head, high_head, low, high, *refs):
-    out, to_next, to_prev, field, wx, kk, ax, axw, py, my, pq, mq, steps, frac = refs[-14:]
+    out, to_next, to_prev, field, other, coarse, wx, kk, ax, axw, py, my, pq, mq, steps, frac = refs[-16:]
 
     def edge_state(i, carry):
         at = pl.ds(pl.multiple_of(8 * i, 8), 8)
-        field[0, i + 2] = low[at, :]
-        field[0, i + 2 + REACH + ROWS] = high[at, :]
+        field[i + 2] = low[at, :]
+        field[i + 2 + REACH + ROWS] = high[at, :]
         return carry
 
     lax.fori_loop(0, REACH, edge_state, 0)
 
     def own_state(r, carry):
         for k in range(PIECES):
-            field[0, r + 2 + REACH, :, lane(k)] = state_row(arrived, half, r, k)
+            field[r + 2 + REACH, :, lane(k)] = state_row(arrived, half, r, k)
         return carry
 
     lax.fori_loop(0, ROWS, own_state, 0)
@@ -217,16 +218,24 @@
 
     def block(substep, source, target, index):
         r = 4 * index + 2
-        tile = (r + 2) // 8
-        f = jnp.where(steps[tile] > substep.astype(WIDE), frac[tile], 0.0)
-        c = {i: split(field[source, r + i]) for i in range(-2, 6)}
-        dx = {i: minus(c[i + 1], c[i]) for i in range(-2, 5)}
-        sx = {i: each(minmod, dx[i], dx[i - 1]) for i in range(-1, 5)}
-        fx = {}
-        for i in range(-1, 4):
-            a = split(ax[r + i] if i >= 0 else axw[index])
-            fx[i] = each(flux, split(wx[r + i]), a, c[i], c[i + 1], sx[i], sx[i + 1])
-        for i in range(4):
+        active = [
+            jnp.where(steps[tile] > substep.astype(WIDE), frac[tile], 0.0)
+            for tile in ((r + 2) // 8, (r + 6) // 8)
+        ]
+        c = {i: split(source[r + i]) for i in (-2, -1, 0, 1)}
+        dx = {i: minus(c[i + 1], c[i]) for i in (-2, -1, 0)}
+        sx = {i: each(minmod, dx[i], dx[i - 1]) for i in (-1, 0)}
+        east = None
+        for i in range(8):
+            c[i + 2] = split(source[r + i + 2])
+            dx[i + 1] = minus(c[i + 2], c[i + 1])
+            sx[i + 1] = each(minmod, dx[i + 1], dx[i])
+            west = east
+            if i % 4 == 0:
+                a = split(axw[index + i // 4])
+                west = each(flux, split(wx[r + i - 1]), a, c[i - 1], c[i], sx[i - 1], sx[i])
+            a = split(ax[r + i])
+            east = each(flux, split(wx[r + i]), a, c[i], c[i + 1], sx[i], sx[i + 1])
             dy = minus(from_right(c[i]), c[i])
             dy_left = minus(c[i], from_left(c[i]))
             sy = each(minmod, dy, dy_left)
@@ -238,34 +247,15 @@
             for p in range(PIECES):
                 spread = (dx[i][p] - dx[i - 1][p]) + (dy[p] - dy_left[p])
                 along = (north_left[p] - north[p]) + (south[p] - south_right[p])
-                rate = (fx[i - 1][p] - fx[i][p]) + along + k_row[p] * spread
-                field[target, r + i, :, lane(p)] = c[i][p] + f * rate
-
-    def substep_blocks(substep, carry):
-        source = jnp.where(substep == 0, 0, 1 + (substep + 1) % 2)
-        target = 1 + substep % 2
-        first = (substep + 1) // 2
-        lax.fori_loop(
-            first,
-            EXT // 4 - first,
-            lambda index, _: block(substep, source, target, index),
-            None,
-        )
-        return carry
-
-    lax.fori_loop(0, SUB, substep_blocks, 0)
-    final = 1 + (SUB - 1) % 2
-    if half == 0:
-        later = jnp.where(lax.broadcasted_iota(jnp.int32, (8, LANE), 0) > 0, 1.0, 0.0)
-    else:
-        later = jnp.ones((8, LANE), WIDE)
+                rate = (west[p] - east[p]) + along + k_row[p] * spread
+                target[r + i, :, lane(p)] = c[i][p] + active[i // 4] * rate
 
     def upwind(w, here, there):
         return w * jnp.where(w > 0.0, here, there)
 
-    def compare(index, carry):
+    def coarse_rows(index, carry):
         r = 2 * index + REACH + 2
-        c = {j: split(field[0, r + j]) for j in range(-1, 3)}
+        c = {j: split(field[r + j]) for j in range(-1, 3)}
         fx = [each(upwind, split(wx[r + j]), c[j], c[j + 1]) for j in (-1, 0, 1)]
         for j in range(2):
             right = from_right(c[j])
@@ -274,18 +264,43 @@
             south = each(lambda a, b: a * b, split(my[r + j]), c[j])
             north_left = from_left(north)
             south_right = from_right(south)
-            end = split(field[final, r + j])
             k_row = split(kk[r + j])
-            i = 2 * index + j
             for p in range(PIECES):
                 spread = c[j - 1][p] + c[j + 1][p] + left[p] + right[p] - 4.0 * c[j][p]
                 along = (north_left[p] - north[p]) + (south[p] - south_right[p])
-                coarse = c[j][p] + (fx[j][p] - fx[j + 1][p]) + along + k_row[p] * spread
+                coarse[2 * index + j, :, lane(p)] = (
+                    c[j][p] + (fx[j][p] - fx[j + 1][p]) + along + k_row[p] * spread
+                )
+        return carry
+
+    lax.fori_loop(0, ROWS // 2, coarse_rows, 0)
+
+    def two_substeps(j, carry):
+        for odd, source, target in ((0, field, other), (1, other, field)):
+            lax.fori_loop(
+                0,
+                5 - j - odd,
+                lambda i, _: block(2 * j + odd, source, target, j + odd + 2 * i),
+                None,
+            )
+        return carry
+
+    lax.fori_loop(0, SUB // 2, two_substeps, 0)
+    if half == 0:
+        later = jnp.where(lax.broadcasted_iota(jnp.int32, (8, LANE), 0) > 0, 1.0, 0.0)
+    else:
+        later = jnp.ones((8, LANE), WIDE)
+
+    def finish(index, carry):
+        for j in range(4):
+            i = 4 * index + j
+            for p in range(PIECES):
                 at = (i // 8) * 32 + 8 * p + i % 8
-                out[pl.ds(at, 8, stride=64), :] = end[p] - later * coarse
+                end = field[REACH + 2 + i, :, lane(p)]
+                out[pl.ds(at, 8, stride=64), :] = end - later * coarse[i, :, lane(p)]
         return carry
 
-    lax.fori_loop(0, ROWS // 2, compare, 0)
+    lax.fori_loop(0, ROWS // 4, finish, 0)
 
     to_next[0:8, :] = jnp.zeros((8, Y), WIDE)
     used = next_offset(8 * half + 7) + 8 - 8 * half
@@ -444,8 +459,12 @@
     (sent,) = call(
         prepare_kernel,
         [(TR * LEV, CHUNK, LANE)],
-        "shhhh",
-        scratch=[pltpu.VMEM((LEV, 104, LANE), WIDE), pltpu.SemaphoreType.DMA((4,))],
+        "hhhhh",
+        scratch=[
+            pltpu.VMEM((LEV, 104, LANE), WIDE),
+            pltpu.VMEM((1, 1), jnp.int32),
+            pltpu.SemaphoreType.DMA((5,)),
+        ],
         flops=300000,
         nbytes=2000000,
         vmem=63 << 20,
@@ -465,7 +484,9 @@
 
     rows = pltpu.VMEM((EXT + 4, 8, Y), WIDE)
     scratch = [
-        pltpu.VMEM((3, EXT + 4, 8, Y), WIDE),
+        rows,
+        rows,
+        pltpu.VMEM((ROWS, 8, Y), WIDE),
         rows,
         rows,
         rows,

time: 95.9 us -> 92.1 us (0.960)
  Pallas kernels: 24.9 us -> 21.2 us
    pallas_call x1, Pallas kernels: 10.7 us -> 8.8 us  [on_device(): call(functools.partial(fine_kernel, 0), [(512, LANE), (104, Y), (104, Y)]...]
    pallas_call x1, Pallas kernels: 10.7 us -> 8.8 us  [on_device(): call(functools.partial(fine_kernel, 1), [(512, LANE), (40, Y), (40, Y)],...]
  transfers between devices with their start and end apart: 8 -> 8, of which waited for: 3 -> 3; matrix products, arithmetic and copies ran while one was open for 0% -> 0% of each run, Pallas kernels for 23% -> 20%
where the time goes in v2:
time: 92.1 us; the launch traced here: 91.6 us
  blocking collectives  39.1 us (42%)
  starting transfers between devices  24.7 us (27%)
  Pallas kernels  21.2 us (23%)
  waiting for transfers between devices  5.1 us (6%)
    ppermute x8, starting transfers between devices, to_chip(): return lax.ppermute(array, AXES, route)  24.7 us
    all_to_all x1, blocking collectives, on_device(): arrived = lax.all_to_all(sent, ('slab', 'core'), 0, 0, tiled=True)  20.7 us
    all_to_all x1, blocking collectives, on_device(): lax.all_to_all(chain.reshape(SLABS * 2, 8, Y), ('slab', 'core'), 0, 0, ti...  18.4 us
    pallas_call x1, Pallas kernels, on_device(): call(functools.partial(fine_kernel, 0), [(512, LANE), (104, Y), (104, Y)]...  8.8 us
    pallas_call x1, Pallas kernels, on_device(): call(functools.partial(fine_kernel, 1), [(512, LANE), (40, Y), (40, Y)],...  8.8 us
    ppermute x8, waiting for transfers between devices, to_chip(): return lax.ppermute(array, AXES, route)  5.1 us
    pallas_call x1, Pallas kernels, on_device(): call(prepare_kernel, [(TR * LEV, CHUNK, LANE)], 'hhhhh', scratch=[pltpu.V...  2.11 us
  transfers between devices with their start and end apart: 8, of which 3 were waited for; matrix products, arithmetic and copies ran while one was open for 0% of the time, Pallas kernels for 20%

profile of v2, /device:TPU:97, one launch (start us, length us, event | category | flops | bytes accessed | tf_op | source)
XLA Modules:
  0.0 91.6 jit_solution(13607484464759771172)
XLA Ops:
  0.7 2.1 %shard_map.55 = f32[32,40,128]{2,1,0:T(8,128)} custom-call(s32[1,1]{1,0:T(1,128)S(6)} %copy.7.count_ref, f32[32,32,128]{2,1,0:T(8,128)} %bitcast.41, f32[8,32,128]{2,1,0:T(8,128)} %bitcast.42, f32[8,32,128]{2,1,0:T(8,128)} %bitcast.43, f32[8,32,128]{2,1,0:T(8,128)} %bitcast.44), custom_call_target="tpu_custom_call" | custom-call | flops 300000 | bytes 2000000 | tf_op jit(solution)/shard_map/pallas_call | solution.py:459
  2.8 20.7 %all_to_all.10 = f32[32,40,128]{2,1,0:T(8,128)S(1)} all-to-all(f32[32,40,128]{2,1,0:T(8,128)} %shard_map.55), channel_id=1, replica_groups=mesh['slab'=16,'z'=16,'core'=2] {'slab','core'}, dimensions={0} | all-to-all | bytes 1310720 | tf_op jit(solution)/shard_map/all_to_all | solution.py:472
  23.5 0.1 shard_map.56
  23.6 1.9 %collective-permute-start.1 = (f32[152,512]{1,0:T(8,128)S(1)}, f32[152,512]{1,0:T(8,128)S(1)}, u32[]{:S(2)}, u32[]{:S(2)}) collective-permute-start(f32[152,512]{1,0:T(8,128)S(1)} %get-tuple-element.19), channel_id=1, source_target_pairs={{2,0},{3,1},{4,2},{5,3},{6,4},{7,5},{8,6},{9,7},{10,8},{11,9},{12,... | collective-permute-start | bytes 933896 | tf_op jit(solution)/shard_map/ppermute | solution.py:450
  25.5 4.8 %collective-permute-start = (f32[152,512]{1,0:T(8,128)S(1)}, f32[152,512]{1,0:T(8,128)S(1)}, u32[]{:S(2)}, u32[]{:S(2)}) collective-permute-start(f32[152,512]{1,0:T(8,128)S(1)} %get-tuple-element.18.refs_0_.mine), channel_id=1, source_target_pairs={{0,2},{1,3},{2,4},{3,5},{4,6},{5,7},{6,8},{7,9},{8,10},{9,11},{10,... | collective-permute-start | bytes 933896 | tf_op jit(solution)/shard_map/ppermute | solution.py:450
  30.3 0.1 shard_map.57
  30.4 3.5 %collective-permute-start.2 = (f32[96,512]{1,0:T(8,128)S(1)}, f32[96,512]{1,0:T(8,128)S(1)}, u32[]{:S(2)}, u32[]{:S(2)}) collective-permute-start(f32[96,512]{1,0:T(8,128)S(1)} %get-tuple-element.20), channel_id=1, source_target_pairs={{0,2},{1,3},{2,4},{3,5},{4,6},{5,7},{6,8},{7,9},{8,10},{9,11},{10,... | collective-permute-start | bytes 589832 | tf_op jit(solution)/shard_map/ppermute | solution.py:450
  33.9 1.9 %collective-permute-start.3 = (f32[96,512]{1,0:T(8,128)S(1)}, f32[96,512]{1,0:T(8,128)S(1)}, u32[]{:S(2)}, u32[]{:S(2)}) collective-permute-start(f32[96,512]{1,0:T(8,128)S(1)} %get-tuple-element.21), channel_id=1, source_target_pairs={{2,0},{3,1},{4,2},{5,3},{6,4},{7,5},{8,6},{9,7},{10,8},{11,9},{12,... | collective-permute-start | bytes 589832 | tf_op jit(solution)/shard_map/ppermute | solution.py:450
  35.9 0.3 collective-permute-done.1.high_head.high
  36.2 1.0 %collective-permute-done.low_head.low = f32[152,512]{1,0:T(8,128)S(1)} collective-permute-done((f32[152,512]{1,0:T(8,128)S(1)}, f32[152,512]{1,0:T(8,128)S(1)}, u32[]{:S(2)}, u32[]{:S(2)}) %collective-permute-start) | collective-permute-done | bytes 311328 | tf_op jit(solution)/shard_map/ppermute | solution.py:450
  37.2 8.8 %shard_map.58 = (f32[512,128]{1,0:T(8,128)S(1)}, f32[104,512]{1,0:T(8,128)S(1)}, f32[104,512]{1,0:T(8,128)S(1)}) custom-call(f32[1280,128]{1,0:T(8,128)S(1)} %bitcast.35, f32[152,512]{1,0:T(8,128)S(1)} %get-tuple-element.18.refs_0_.mine, f32[152,512]{1,0:T(8,128)S(1)} %collective-permute-done.low_head.low, ...), custom_call_target="tpu_custom_call" | custom-call | flops 25000000 | bytes 3000000 | tf_op jit(solution)/shard_map/pallas_call | solution.py:501
  46.0 1.9 %collective-permute-start.7 = (f32[104,512]{1,0:T(8,128)S(1)}, f32[104,512]{1,0:T(8,128)S(1)}, u32[]{:S(2)}, u32[]{:S(2)}) collective-permute-start(f32[104,512]{1,0:T(8,128)S(1)} %get-tuple-element.27), channel_id=1, source_target_pairs={{2,0},{3,1},{4,2},{5,3},{6,4},{7,5},{8,6},{9,7},{10,8},{11,9},{12,... | collective-permute-start | bytes 638984 | tf_op jit(solution)/shard_map/ppermute | solution.py:450
  47.9 5.3 %collective-permute-start.6 = (f32[104,512]{1,0:T(8,128)S(1)}, f32[104,512]{1,0:T(8,128)S(1)}, u32[]{:S(2)}, u32[]{:S(2)}) collective-permute-start(f32[104,512]{1,0:T(8,128)S(1)} %get-tuple-element.22.refs_0_), channel_id=1, source_target_pairs={{0,2},{1,3},{2,4},{3,5},{4,6},{5,7},{6,8},{7,9},{8,10},{9,11},{10,... | collective-permute-start | bytes 638984 | tf_op jit(solution)/shard_map/ppermute | solution.py:450
  53.2 0.0 collective-permute-done.2.low
  53.2 0.0 collective-permute-done.3.high
  53.2 8.8 %shard_map.59 = (f32[512,128]{1,0:T(8,128)S(1)}, f32[40,512]{1,0:T(8,128)S(1)}, f32[40,512]{1,0:T(8,128)S(1)}) custom-call(f32[1280,128]{1,0:T(8,128)S(1)} %bitcast.36, f32[152,512]{1,0:T(8,128)S(1)} %get-tuple-element.18.refs_0_.mine, f32[152,512]{1,0:T(8,128)S(1)} %collective-permute-done.low_head.low, ...), custom_call_target="tpu_custom_call" | custom-call | flops 25000000 | bytes 3000000 | tf_op jit(solution)/shard_map/pallas_call | solution.py:510
  62.0 3.4 %collective-permute-start.4 = (f32[40,512]{1,0:T(8,128)S(1)}, f32[40,512]{1,0:T(8,128)S(1)}, u32[]{:S(2)}, u32[]{:S(2)}) collective-permute-start(f32[40,512]{1,0:T(8,128)S(1)} %get-tuple-element.24), channel_id=1, source_target_pairs={{0,2},{1,3},{2,4},{3,5},{4,6},{5,7},{6,8},{7,9},{8,10},{9,11},{10,... | collective-permute-start | bytes 245768 | tf_op jit(solution)/shard_map/ppermute | solution.py:450
  65.4 1.9 %collective-permute-start.5 = (f32[40,512]{1,0:T(8,128)S(1)}, f32[40,512]{1,0:T(8,128)S(1)}, u32[]{:S(2)}, u32[]{:S(2)}) collective-permute-start(f32[40,512]{1,0:T(8,128)S(1)} %get-tuple-element.25), channel_id=1, source_target_pairs={{2,0},{3,1},{4,2},{5,3},{6,4},{7,5},{8,6},{9,7},{10,8},{11,9},{12,... | collective-permute-start | bytes 245768 | tf_op jit(solution)/shard_map/ppermute | solution.py:450
  67.3 0.0 collective-permute-done.7.high
  67.4 0.0 collective-permute-done.6.low
  67.4 0.6 shard_map.60
  68.0 0.0 collective-permute-done.4.low
  68.0 3.8 %collective-permute-done.5.high = f32[40,512]{1,0:T(8,128)S(1)} collective-permute-done((f32[40,512]{1,0:T(8,128)S(1)}, f32[40,512]{1,0:T(8,128)S(1)}, u32[]{:S(2)}, u32[]{:S(2)}) %collective-permute-start.5) | collective-permute-done | bytes 81952 | tf_op jit(solution)/shard_map/ppermute | solution.py:450
  71.8 0.6 shard_map.61
  72.4 18.4 %all_to_all.11 = f32[32,8,512]{2,1,0:T(8,128)S(1)} all-to-all(f32[32,8,512]{2,1,0:T(8,128)S(1)} %bitcast.37), channel_id=1, replica_groups=mesh['slab'=16,'z'=16,'core'=2] {'slab','core'}, dimensions={0} | all-to-all | bytes 1048576 | tf_op jit(solution)/shard_map/all_to_all | solution.py:526
  90.8 0.8 copy.8
Async XLA Ops:
  23.6 12.6 %collective-permute-start.1 = (f32[152,512]{1,0:T(8,128)S(1)}, f32[152,512]{1,0:T(8,128)S(1)}, u32[]{:S(2)}, u32[]{:S(2)}) collective-permute-start(f32[152,512]{1,0:T(8,128)S(1)} %get-tuple-element.19), channel_id=1, source_target_pairs={{2,0},{3,1},{4,2},{5,3},{6,4},{7,5},{8,6},{9,7},{10,8},{11,9},{12,... | collective-permute-start | bytes 933896 | tf_op jit(solution)/shard_map/ppermute | solution.py:450
  25.5 11.6 %collective-permute-start = (f32[152,512]{1,0:T(8,128)S(1)}, f32[152,512]{1,0:T(8,128)S(1)}, u32[]{:S(2)}, u32[]{:S(2)}) collective-permute-start(f32[152,512]{1,0:T(8,128)S(1)} %get-tuple-element.18.refs_0_.mine), channel_id=1, source_target_pairs={{0,2},{1,3},{2,4},{3,5},{4,6},{5,7},{6,8},{7,9},{8,10},{9,11},{10,... | collective-permute-start | bytes 933896 | tf_op jit(solution)/shard_map/ppermute | solution.py:450
  30.4 22.8 %collective-permute-start.2 = (f32[96,512]{1,0:T(8,128)S(1)}, f32[96,512]{1,0:T(8,128)S(1)}, u32[]{:S(2)}, u32[]{:S(2)}) collective-permute-start(f32[96,512]{1,0:T(8,128)S(1)} %get-tuple-element.20), channel_id=1, source_target_pairs={{0,2},{1,3},{2,4},{3,5},{4,6},{5,7},{6,8},{7,9},{8,10},{9,11},{10,... | collective-permute-start | bytes 589832 | tf_op jit(solution)/shard_map/ppermute | solution.py:450
  33.9 19.3 %collective-permute-start.3 = (f32[96,512]{1,0:T(8,128)S(1)}, f32[96,512]{1,0:T(8,128)S(1)}, u32[]{:S(2)}, u32[]{:S(2)}) collective-permute-start(f32[96,512]{1,0:T(8,128)S(1)} %get-tuple-element.21), channel_id=1, source_target_pairs={{2,0},{3,1},{4,2},{5,3},{6,4},{7,5},{8,6},{9,7},{10,8},{11,9},{12,... | collective-permute-start | bytes 589832 | tf_op jit(solution)/shard_map/ppermute | solution.py:450
  46.0 21.4 %collective-permute-start.7 = (f32[104,512]{1,0:T(8,128)S(1)}, f32[104,512]{1,0:T(8,128)S(1)}, u32[]{:S(2)}, u32[]{:S(2)}) collective-permute-start(f32[104,512]{1,0:T(8,128)S(1)} %get-tuple-element.27), channel_id=1, source_target_pairs={{2,0},{3,1},{4,2},{5,3},{6,4},{7,5},{8,6},{9,7},{10,8},{11,9},{12,... | collective-permute-start | bytes 638984 | tf_op jit(solution)/shard_map/ppermute | solution.py:450
  47.9 19.5 %collective-permute-start.6 = (f32[104,512]{1,0:T(8,128)S(1)}, f32[104,512]{1,0:T(8,128)S(1)}, u32[]{:S(2)}, u32[]{:S(2)}) collective-permute-start(f32[104,512]{1,0:T(8,128)S(1)} %get-tuple-element.22.refs_0_), channel_id=1, source_target_pairs={{0,2},{1,3},{2,4},{3,5},{4,6},{5,7},{6,8},{7,9},{8,10},{9,11},{10,... | collective-permute-start | bytes 638984 | tf_op jit(solution)/shard_map/ppermute | solution.py:450
  62.0 6.0 %collective-permute-start.4 = (f32[40,512]{1,0:T(8,128)S(1)}, f32[40,512]{1,0:T(8,128)S(1)}, u32[]{:S(2)}, u32[]{:S(2)}) collective-permute-start(f32[40,512]{1,0:T(8,128)S(1)} %get-tuple-element.24), channel_id=1, source_target_pairs={{0,2},{1,3},{2,4},{3,5},{4,6},{5,7},{6,8},{7,9},{8,10},{9,11},{10,... | collective-permute-start | bytes 245768 | tf_op jit(solution)/shard_map/ppermute | solution.py:450
  65.4 6.4 %collective-permute-start.5 = (f32[40,512]{1,0:T(8,128)S(1)}, f32[40,512]{1,0:T(8,128)S(1)}, u32[]{:S(2)}, u32[]{:S(2)}) collective-permute-start(f32[40,512]{1,0:T(8,128)S(1)} %get-tuple-element.25), channel_id=1, source_target_pairs={{2,0},{3,1},{4,2},{5,3},{6,4},{7,5},{8,6},{9,7},{10,8},{11,9},{12,... | collective-permute-start | bytes 245768 | tf_op jit(solution)/shard_map/ppermute | solution.py:450

commit v3 on v2

--- a/solution.py
+++ b/solution.py
@@ -18,6 +18,7 @@
 EXT = ROWS + 2 * REACH
 CHUNK = 40
 STATE = 8 * REACH
+WIDE_HALO, NARROW_HALO = 104, 40
 WIDE = jnp.float32
 AXES = ("slab", "z", "core")
 
@@ -152,22 +153,7 @@
 
 
 def fine_kernel(half, arrived, mine, low_head, high_head, low, high, *refs):
-    out, to_next, to_prev, field, other, coarse, wx, kk, ax, axw, py, my, pq, mq, steps, frac = refs[-16:]
-
-    def edge_state(i, carry):
-        at = pl.ds(pl.multiple_of(8 * i, 8), 8)
-        field[i + 2] = low[at, :]
-        field[i + 2 + REACH + ROWS] = high[at, :]
-        return carry
-
-    lax.fori_loop(0, REACH, edge_state, 0)
-
-    def own_state(r, carry):
-        for k in range(PIECES):
-            field[r + 2 + REACH, :, lane(k)] = state_row(arrived, half, r, k)
-        return carry
-
-    lax.fori_loop(0, ROWS, own_state, 0)
+    field, other, coarse, wx, kk, ax, axw, py, my, pq, mq, steps, frac = refs[-13:]
     for tile in range(6):
         ref = (low_head, mine, high_head)[tile // 2]
         at = STATE + 48
@@ -175,39 +161,42 @@
         steps[tile] = number
         frac[tile] = 1.0 / jnp.maximum(number, 1.0)
 
-    def spread_rows(ref, first, shift):
-        def one(i, carry):
-            for q, target in enumerate((wx, py, kk)):
-                row = ref[pl.ds(STATE + 16 * q + first + i, 1), :]
-                target[i + first + shift] = jnp.broadcast_to(row, (8, Y))
-            return carry
-
-        return one
-
-    lax.fori_loop(0, REACH, spread_rows(low_head, ROWS - REACH, REACH + 2 - ROWS), 0)
-    lax.fori_loop(0, ROWS, spread_rows(mine, 0, REACH + 2), 0)
-    lax.fori_loop(0, REACH, spread_rows(high_head, 0, REACH + ROWS + 2), 0)
-
     def limited(size, half_fraction):
         return size * (0.5 - half_fraction * size)
 
-    def coefficients(i, carry):
-        r = 4 * i + 2
-        part = 0.5 * frac[(r + 2) // 8]
-        half_fraction = join([part] * PIECES)
-        axw[i] = limited(jnp.abs(wx[r - 1]), half_fraction)
-        for j in range(4):
-            ax[r + j] = limited(jnp.abs(wx[r + j]), half_fraction)
-            north = py[r + j]
-            south = join(from_left(split(north)))
-            forward, backward = jnp.maximum(north, 0.0), jnp.minimum(south, 0.0)
-            py[r + j] = forward
-            my[r + j] = backward
-            pq[r + j] = limited(forward, half_fraction)
-            mq[r + j] = limited(-backward, half_fraction)
-        return carry
-
-    lax.fori_loop(0, EXT // 4, coefficients, 0)
+    def set_up(head, states, first, groups, row):
+        def group_rows(i, carry):
+            group = first + i
+            r = 4 * group + 2
+            part = 0.5 * frac[(r + 2) // 8]
+            half_fraction = join([part] * PIECES)
+            axw[group] = limited(jnp.abs(wx[r - 1]), half_fraction)
+            for j in range(4):
+                if states is None:
+                    for k in range(PIECES):
+                        field[r + j, :, lane(k)] = state_row(arrived, half, 4 * i + j, k)
+                else:
+                    field[r + j] = states[pl.ds(pl.multiple_of(32 * i + 8 * j, 8), 8), :]
+                east, north, spread = [
+                    jnp.broadcast_to(head[pl.ds(STATE + 16 * q + row + 4 * i + j, 1), :], (8, Y))
+                    for q in range(3)
+                ]
+                wx[r + j] = east
+                kk[r + j] = spread
+                ax[r + j] = limited(jnp.abs(east), half_fraction)
+                south = join(from_left(split(north)))
+                forward, backward = jnp.maximum(north, 0.0), jnp.minimum(south, 0.0)
+                py[r + j] = forward
+                my[r + j] = backward
+                pq[r + j] = limited(forward, half_fraction)
+                mq[r + j] = limited(-backward, half_fraction)
+            return carry
+
+        lax.fori_loop(0, groups, group_rows, 0)
+
+    set_up(low_head, low, 0, REACH // 4, ROWS - REACH)
+    set_up(mine, None, REACH // 4, ROWS // 4, 0)
+    set_up(high_head, high, (REACH + ROWS) // 4, REACH // 4, 0)
 
     def flux(w, a, here, there, slope_here, slope_there):
         up = w > 0.0
@@ -254,10 +243,10 @@
         return w * jnp.where(w > 0.0, here, there)
 
     def coarse_rows(index, carry):
-        r = 2 * index + REACH + 2
-        c = {j: split(field[r + j]) for j in range(-1, 3)}
-        fx = [each(upwind, split(wx[r + j]), c[j], c[j + 1]) for j in (-1, 0, 1)]
-        for j in range(2):
+        r = 4 * index + REACH + 2
+        c = {j: split(field[r + j]) for j in range(-1, 5)}
+        fx = [each(upwind, split(wx[r + j]), c[j], c[j + 1]) for j in range(-1, 4)]
+        for j in range(4):
             right = from_right(c[j])
             left = from_left(c[j])
             north = each(lambda a, b: a * b, split(py[r + j]), c[j])
@@ -268,12 +257,12 @@
             for p in range(PIECES):
                 spread = c[j - 1][p] + c[j + 1][p] + left[p] + right[p] - 4.0 * c[j][p]
                 along = (north_left[p] - north[p]) + (south[p] - south_right[p])
-                coarse[2 * index + j, :, lane(p)] = (
+                coarse[4 * index + j, :, lane(p)] = (
                     c[j][p] + (fx[j][p] - fx[j + 1][p]) + along + k_row[p] * spread
                 )
         return carry
 
-    lax.fori_loop(0, ROWS // 2, coarse_rows, 0)
+    lax.fori_loop(0, ROWS // 4, coarse_rows, 0)
 
     def two_substeps(j, carry):
         for odd, source, target in ((0, field, other), (1, other, field)):
@@ -286,6 +275,7 @@
         return carry
 
     lax.fori_loop(0, SUB // 2, two_substeps, 0)
+    out = refs[0] if half == 0 else refs[1]
     if half == 0:
         later = jnp.where(lax.broadcasted_iota(jnp.int32, (8, LANE), 0) > 0, 1.0, 0.0)
     else:
@@ -301,12 +291,19 @@
         return carry
 
     lax.fori_loop(0, ROWS // 4, finish, 0)
-
-    to_next[0:8, :] = jnp.zeros((8, Y), WIDE)
+    if half:
+        earlier, _, to_next, to_prev = refs[:4]
+        pack(0, earlier, to_next, to_prev)
+        pack(1, out, to_next, to_prev)
+
+
+def pack(half, out, to_next, to_prev):
+    base = WIDE_HALO * half
+    to_next[base : base + 8, :] = jnp.zeros((8, Y), WIDE)
     used = next_offset(8 * half + 7) + 8 - 8 * half
+    total = NARROW_HALO if half else WIDE_HALO
     for ref, filled in ((to_next, used), (to_prev, used - 8)):
-        total = ref.shape[0]
-        ref[filled:total, :] = jnp.zeros((total - filled, Y), WIDE)
+        ref[base + filled : base + total, :] = jnp.zeros((total - filled, Y), WIDE)
     for n in range(8 * half, min(8 * half + 8, 15)):
         rows = 15 - n
         for k in range(PIECES):
@@ -315,13 +312,13 @@
                 at = (2 * (n - 8 * half) + upper) * 32 + 8 * k
                 return out[at + first : at + last, :]
 
-            at = next_offset(n)
+            at = base + next_offset(n)
             if rows > 8:
                 to_next[at : at + rows - 8, lane(k)] = piece(16 - rows, 8, 0)
                 to_next[at + rows - 8 : at + rows, lane(k)] = piece(0, 8, 1)
             else:
                 to_next[at : at + rows, lane(k)] = piece(8 - rows, 8, 1)
-            at = prev_offset(n)
+            at = base + prev_offset(n)
             if rows > 8:
                 to_prev[at : at + 8, lane(k)] = piece(0, 8, 0)
                 to_prev[at + 8 : at + rows, lane(k)] = piece(0, rows - 8, 1)
@@ -354,14 +351,15 @@
 
 def differences(half, n, own, low, high):
     size = 8 if half else 16
+    base = WIDE_HALO * half
     tiles = []
     if n < 15:
-        at = next_offset(n) + 15 - n - size
+        at = base + next_offset(n) + 15 - n - size
         tiles += [rows_at(low, at + 8 * k) for k in range(size // 8)]
     at = 16 * (n - 8 * half)
     tiles += [rows_at(own, at), rows_at(own, at + 8)]
     if n < 15:
-        at = prev_offset(n)
+        at = base + prev_offset(n)
         tiles += [rows_at(high, at + 8 * k) for k in range(size // 8)]
     return tiles
 
@@ -387,7 +385,7 @@
     return result
 
 
-def first_chain_kernel(own, mine, low_head, high_head, low, high, out, stencil, state):
+def chain_kernel(own, later, mine, low_head, high_head, low, high, out, stencil):
     inside = jnp.where(lax.axis_index("z") < CHIPS - 1, 1.0, 0.0).astype(WIDE)
 
     def rows_of(q):
@@ -418,16 +416,9 @@
             value = advance(value, 0, differences(0, n, own, low, high), stencil, inside)
         for k in range(2):
             out[16 * n + 8 * k : 16 * n + 8 * k + 8, :] = join(value[k + 2])
-    for k in range(4):
-        state[8 * k : 8 * k + 8, :] = join(value[k + 1])
-
-
-def second_chain_kernel(own, low, high, done, stencil, state, out):
-    inside = jnp.where(lax.axis_index("z") < CHIPS - 1, 1.0, 0.0).astype(WIDE)
-    out[0:128, :] = done[...]
-    value = [rows_at(state, 8 * k) for k in range(4)]
+    value = value[1:5]
     for n in range(8, 16):
-        added = differences(1, n, own, low, high)
+        added = differences(1, n, later, low, high)
         keep = slice(1, 3) if n == 15 else None
         value = advance(value, 1, added, stencil, inside, keep)
         for k in range(2):
@@ -498,31 +489,31 @@
         pltpu.VMEM((6, 8, LANE), WIDE),
         pltpu.VMEM((6, 8, LANE), WIDE),
     ]
-    own_a, next_c, prev_c = call(
+    (own_a,) = call(
         functools.partial(fine_kernel, 0),
-        [(512, LANE), (104, Y), (104, Y)],
+        [(512, LANE)],
         "vvvvvv",
         scratch=scratch,
         flops=25000000,
         nbytes=3000000,
     )(arrived, next_a, low_a, high_a, low_a, high_a)
-    low_c, high_c = to_chip(next_c, 1), to_chip(prev_c, -1)
-    own_b, next_d, prev_d = call(
+    halo = (WIDE_HALO + NARROW_HALO, Y)
+    own_b, next_c, prev_c = call(
         functools.partial(fine_kernel, 1),
-        [(512, LANE), (40, Y), (40, Y)],
-        "vvvvvvh",
+        [(512, LANE), halo, halo],
+        "vvvvvvv",
         scratch=scratch,
         flops=25000000,
         nbytes=3000000,
-    )(arrived, next_a, low_a, high_a, low_b, high_b, next_c)
-    low_d, high_d = to_chip(next_d, 1), to_chip(prev_d, -1)
-    own_a, own_b = [from_tiles(a) for a in (own_a, own_b)]
-    done, stencil, state = call(
-        first_chain_kernel, [(128, Y), (5, 48, Y), (32, Y)], "vvvvvv", flops=5000000
-    )(own_a, next_a, low_a, high_a, low_c, high_c)
-    (chain,) = call(second_chain_kernel, [(256, Y)], "vvvvvv", flops=3000000)(
-        own_b, low_d, high_d, done, stencil, state
-    )
+    )(arrived, next_a, low_a, high_a, low_b, high_b, own_a)
+    low_c, high_c = to_chip(next_c, 1), to_chip(prev_c, -1)
+    (chain,) = call(
+        chain_kernel,
+        [(256, Y)],
+        "vvvvvvv",
+        scratch=[pltpu.VMEM((5, 48, Y), WIDE)],
+        flops=8000000,
+    )(from_tiles(own_a), from_tiles(own_b), next_a, low_a, high_a, low_c, high_c)
     result = lax.all_to_all(
         chain.reshape(SLABS * 2, 8, Y), ("slab", "core"), 0, 0, tiled=True
     )

time: 92.1 us -> 88.3 us (0.959)
  the two profiles are of different devices: /device:TPU:97 before, /device:TPU:225 now
where the time goes in v3:
time: 88.3 us; the launch traced here: 87.9 us
  blocking collectives  37.6 us (43%)
  Pallas kernels  19.7 us (22%)
  starting transfers between devices  19.2 us (22%)
  waiting for transfers between devices  9.86 us (11%)
    all_to_all x1, blocking collectives, on_device(): arrived = lax.all_to_all(sent, ('slab', 'core'), 0, 0, tiled=True)  20.7 us
    ppermute x6, starting transfers between devices, to_chip(): return lax.ppermute(array, AXES, route)  19.2 us
    all_to_all x1, blocking collectives, on_device(): lax.all_to_all(chain.reshape(SLABS * 2, 8, Y), ('slab', 'core'), 0, 0, ti...  16.9 us
    ppermute x6, waiting for transfers between devices, to_chip(): return lax.ppermute(array, AXES, route)  9.86 us
    pallas_call x1, Pallas kernels, on_device(): call(functools.partial(fine_kernel, 1), [(512, LANE), halo, halo], 'vvvvv...  8.11 us
    pallas_call x1, Pallas kernels, on_device(): call(functools.partial(fine_kernel, 0), [(512, LANE)], 'vvvvvv', scratch=...  8.02 us
    pallas_call x1, Pallas kernels, on_device(): call(prepare_kernel, [(TR * LEV, CHUNK, LANE)], 'hhhhh', scratch=[pltpu.V...  2.11 us
  transfers between devices with their start and end apart: 6, of which 4 were waited for; matrix products, arithmetic and copies ran while one was open for 0% of the time, Pallas kernels for 9%

profile of v3, /device:TPU:225, one launch (start us, length us, event | category | flops | bytes accessed | tf_op | source)
XLA Modules:
  0.0 87.9 jit_solution(6208359674000761568)
XLA Ops:
  0.7 2.1 %shard_map.55 = f32[32,40,128]{2,1,0:T(8,128)} custom-call(s32[1,1]{1,0:T(1,128)S(6)} %copy.7.count_ref, f32[32,32,128]{2,1,0:T(8,128)} %bitcast.41, f32[8,32,128]{2,1,0:T(8,128)} %bitcast.42, f32[8,32,128]{2,1,0:T(8,128)} %bitcast.43, f32[8,32,128]{2,1,0:T(8,128)} %bitcast.44), custom_call_target="tpu_custom_call" | custom-call | flops 300000 | bytes 2000000 | tf_op jit(solution)/shard_map/pallas_call | solution.py:450
  2.8 20.7 %all_to_all.10 = f32[32,40,128]{2,1,0:T(8,128)S(1)} all-to-all(f32[32,40,128]{2,1,0:T(8,128)} %shard_map.55), channel_id=1, replica_groups=mesh['slab'=16,'z'=16,'core'=2] {'slab','core'}, dimensions={0} | all-to-all | bytes 1310720 | tf_op jit(solution)/shard_map/all_to_all | solution.py:463
  23.5 0.1 shard_map.56
  23.6 1.9 %collective-permute-start.1 = (f32[152,512]{1,0:T(8,128)S(1)}, f32[152,512]{1,0:T(8,128)S(1)}, u32[]{:S(2)}, u32[]{:S(2)}) collective-permute-start(f32[152,512]{1,0:T(8,128)S(1)} %get-tuple-element.13), channel_id=1, source_target_pairs={{2,0},{3,1},{4,2},{5,3},{6,4},{7,5},{8,6},{9,7},{10,8},{11,9},{12,... | collective-permute-start | bytes 933896 | tf_op jit(solution)/shard_map/ppermute | solution.py:441
  25.5 4.8 %collective-permute-start = (f32[152,512]{1,0:T(8,128)S(1)}, f32[152,512]{1,0:T(8,128)S(1)}, u32[]{:S(2)}, u32[]{:S(2)}) collective-permute-start(f32[152,512]{1,0:T(8,128)S(1)} %get-tuple-element.12.mine.refs_0_), channel_id=1, source_target_pairs={{0,2},{1,3},{2,4},{3,5},{4,6},{5,7},{6,8},{7,9},{8,10},{9,11},{10,... | collective-permute-start | bytes 933896 | tf_op jit(solution)/shard_map/ppermute | solution.py:441
  30.3 0.1 shard_map.58
  30.4 3.4 %collective-permute-start.2 = (f32[96,512]{1,0:T(8,128)S(1)}, f32[96,512]{1,0:T(8,128)S(1)}, u32[]{:S(2)}, u32[]{:S(2)}) collective-permute-start(f32[96,512]{1,0:T(8,128)S(1)} %get-tuple-element.14), channel_id=1, source_target_pairs={{0,2},{1,3},{2,4},{3,5},{4,6},{5,7},{6,8},{7,9},{8,10},{9,11},{10,... | collective-permute-start | bytes 589832 | tf_op jit(solution)/shard_map/ppermute | solution.py:441
  33.8 1.9 %collective-permute-start.3 = (f32[96,512]{1,0:T(8,128)S(1)}, f32[96,512]{1,0:T(8,128)S(1)}, u32[]{:S(2)}, u32[]{:S(2)}) collective-permute-start(f32[96,512]{1,0:T(8,128)S(1)} %get-tuple-element.15), channel_id=1, source_target_pairs={{2,0},{3,1},{4,2},{5,3},{6,4},{7,5},{8,6},{9,7},{10,8},{11,9},{12,... | collective-permute-start | bytes 589832 | tf_op jit(solution)/shard_map/ppermute | solution.py:441
  35.7 0.5 collective-permute-done.1.high_head.high
  36.2 1.0 %collective-permute-done.low_head.low = f32[152,512]{1,0:T(8,128)S(1)} collective-permute-done((f32[152,512]{1,0:T(8,128)S(1)}, f32[152,512]{1,0:T(8,128)S(1)}, u32[]{:S(2)}, u32[]{:S(2)}) %collective-permute-start) | collective-permute-done | bytes 311328 | tf_op jit(solution)/shard_map/ppermute | solution.py:441
  37.2 8.0 %shard_map.57.refs_0_ = f32[512,128]{1,0:T(8,128)S(1)} custom-call(f32[1280,128]{1,0:T(8,128)S(1)} %bitcast.35, f32[152,512]{1,0:T(8,128)S(1)} %get-tuple-element.12.mine.refs_0_, f32[152,512]{1,0:T(8,128)S(1)} %collective-permute-done.low_head.low, f32[152,512]{1,0:T(8,128)S(1)} %collective-permute-done.1.high_head.high, ...), custom_call_target="tpu_custom_call" | custom-call | flops 25000000 | bytes 3000000 | tf_op jit(solution)/shard_map/pallas_call | solution.py:492
  45.2 0.0 collective-permute-done.2.low
  45.2 0.0 collective-permute-done.3.high
  45.2 8.1 %shard_map.59 = (f32[512,128]{1,0:T(8,128)S(1)}, f32[144,512]{1,0:T(8,128)S(1)}, f32[144,512]{1,0:T(8,128)S(1)}) custom-call(f32[1280,128]{1,0:T(8,128)S(1)} %bitcast.36, f32[152,512]{1,0:T(8,128)S(1)} %get-tuple-element.12.mine.refs_0_, f32[152,512]{1,0:T(8,128)S(1)} %collective-permute-done.low_head.low, ...), custom_call_target="tpu_custom_call" | custom-call | flops 25000000 | bytes 3000000 | tf_op jit(solution)/shard_map/pallas_call | solution.py:501
  53.3 5.3 %collective-permute-start.4 = (f32[144,512]{1,0:T(8,128)S(1)}, f32[144,512]{1,0:T(8,128)S(1)}, u32[]{:S(2)}, u32[]{:S(2)}) collective-permute-start(f32[144,512]{1,0:T(8,128)S(1)} %get-tuple-element.17), channel_id=1, source_target_pairs={{0,2},{1,3},{2,4},{3,5},{4,6},{5,7},{6,8},{7,9},{8,10},{9,11},{10,... | collective-permute-start | bytes 884744 | tf_op jit(solution)/shard_map/ppermute | solution.py:441
  58.6 1.9 %collective-permute-start.5 = (f32[144,512]{1,0:T(8,128)S(1)}, f32[144,512]{1,0:T(8,128)S(1)}, u32[]{:S(2)}, u32[]{:S(2)}) collective-permute-start(f32[144,512]{1,0:T(8,128)S(1)} %get-tuple-element.18), channel_id=1, source_target_pairs={{2,0},{3,1},{4,2},{5,3},{6,4},{7,5},{8,6},{9,7},{10,8},{11,9},{12,... | collective-permute-start | bytes 884744 | tf_op jit(solution)/shard_map/ppermute | solution.py:441
  60.6 3.4 %collective-permute-done.4.low = f32[144,512]{1,0:T(8,128)S(1)} collective-permute-done((f32[144,512]{1,0:T(8,128)S(1)}, f32[144,512]{1,0:T(8,128)S(1)}, u32[]{:S(2)}, u32[]{:S(2)}) %collective-permute-start.4) | collective-permute-done | bytes 294944 | tf_op jit(solution)/shard_map/ppermute | solution.py:441
  63.9 5.0 %collective-permute-done.5.high = f32[144,512]{1,0:T(8,128)S(1)} collective-permute-done((f32[144,512]{1,0:T(8,128)S(1)}, f32[144,512]{1,0:T(8,128)S(1)}, u32[]{:S(2)}, u32[]{:S(2)}) %collective-permute-start.5) | collective-permute-done | bytes 294944 | tf_op jit(solution)/shard_map/ppermute | solution.py:441
  69.0 1.2 %shard_map.60 = f32[256,512]{1,0:T(8,128)S(1)} custom-call(f32[128,512]{1,0:T(8,128)S(1)} %bitcast.37, f32[128,512]{1,0:T(8,128)S(1)} %bitcast.39, f32[152,512]{1,0:T(8,128)S(1)} %get-tuple-element.12.mine.refs_0_, f32[152,512]{1,0:T(8,128)S(1)} %collective-permute-done.low_head.low, f32[152,512]{1,0:T(8,128)S(1)} %collective-permute-done.1.high_head.high, ...), custom_call_target="tpu_custom_call" | custom-call | flops 8000000 | bytes 1000000 | tf_op jit(solution)/shard_map/pallas_call | solution.py:510
  70.2 16.9 %all_to_all.11 = f32[32,8,512]{2,1,0:T(8,128)S(1)} all-to-all(f32[32,8,512]{2,1,0:T(8,128)S(1)} %bitcast.38), channel_id=1, replica_groups=mesh['slab'=16,'z'=16,'core'=2] {'slab','core'}, dimensions={0} | all-to-all | bytes 1048576 | tf_op jit(solution)/shard_map/all_to_all | solution.py:517
  87.1 0.8 copy.8
Async XLA Ops:
  23.6 12.6 %collective-permute-start.1 = (f32[152,512]{1,0:T(8,128)S(1)}, f32[152,512]{1,0:T(8,128)S(1)}, u32[]{:S(2)}, u32[]{:S(2)}) collective-permute-start(f32[152,512]{1,0:T(8,128)S(1)} %get-tuple-element.13), channel_id=1, source_target_pairs={{2,0},{3,1},{4,2},{5,3},{6,4},{7,5},{8,6},{9,7},{10,8},{11,9},{12,... | collective-permute-start | bytes 933896 | tf_op jit(solution)/shard_map/ppermute | solution.py:441
  25.5 11.6 %collective-permute-start = (f32[152,512]{1,0:T(8,128)S(1)}, f32[152,512]{1,0:T(8,128)S(1)}, u32[]{:S(2)}, u32[]{:S(2)}) collective-permute-start(f32[152,512]{1,0:T(8,128)S(1)} %get-tuple-element.12.mine.refs_0_), channel_id=1, source_target_pairs={{0,2},{1,3},{2,4},{3,5},{4,6},{5,7},{6,8},{7,9},{8,10},{9,11},{10,... | collective-permute-start | bytes 933896 | tf_op jit(solution)/shard_map/ppermute | solution.py:441
  30.4 14.8 %collective-permute-start.2 = (f32[96,512]{1,0:T(8,128)S(1)}, f32[96,512]{1,0:T(8,128)S(1)}, u32[]{:S(2)}, u32[]{:S(2)}) collective-permute-start(f32[96,512]{1,0:T(8,128)S(1)} %get-tuple-element.14), channel_id=1, source_target_pairs={{0,2},{1,3},{2,4},{3,5},{4,6},{5,7},{6,8},{7,9},{8,10},{9,11},{10,... | collective-permute-start | bytes 589832 | tf_op jit(solution)/shard_map/ppermute | solution.py:441
  33.8 11.4 %collective-permute-start.3 = (f32[96,512]{1,0:T(8,128)S(1)}, f32[96,512]{1,0:T(8,128)S(1)}, u32[]{:S(2)}, u32[]{:S(2)}) collective-permute-start(f32[96,512]{1,0:T(8,128)S(1)} %get-tuple-element.15), channel_id=1, source_target_pairs={{2,0},{3,1},{4,2},{5,3},{6,4},{7,5},{8,6},{9,7},{10,8},{11,9},{12,... | collective-permute-start | bytes 589832 | tf_op jit(solution)/shard_map/ppermute | solution.py:441
  53.3 10.6 %collective-permute-start.4 = (f32[144,512]{1,0:T(8,128)S(1)}, f32[144,512]{1,0:T(8,128)S(1)}, u32[]{:S(2)}, u32[]{:S(2)}) collective-permute-start(f32[144,512]{1,0:T(8,128)S(1)} %get-tuple-element.17), channel_id=1, source_target_pairs={{0,2},{1,3},{2,4},{3,5},{4,6},{5,7},{6,8},{7,9},{8,10},{9,11},{10,... | collective-permute-start | bytes 884744 | tf_op jit(solution)/shard_map/ppermute | solution.py:441
  58.6 10.3 %collective-permute-start.5 = (f32[144,512]{1,0:T(8,128)S(1)}, f32[144,512]{1,0:T(8,128)S(1)}, u32[]{:S(2)}, u32[]{:S(2)}) collective-permute-start(f32[144,512]{1,0:T(8,128)S(1)} %get-tuple-element.18), channel_id=1, source_target_pairs={{2,0},{3,1},{4,2},{5,3},{6,4},{7,5},{8,6},{9,7},{10,8},{11,9},{12,... | collective-permute-start | bytes 884744 | tf_op jit(solution)/shard_map/ppermute | solution.py:441

commit v4 on v3

--- a/solution.py
+++ b/solution.py
@@ -18,7 +18,7 @@
 EXT = ROWS + 2 * REACH
 CHUNK = 40
 STATE = 8 * REACH
-WIDE_HALO, NARROW_HALO = 104, 40
+FIRST, REST, HALO = STATE + 3 * REACH + 8, STATE + 3 * (ROWS - REACH), 128
 WIDE = jnp.float32
 AXES = ("slab", "z", "core")
 
@@ -122,7 +122,12 @@
             to_next[8 * i : 8 * i + 8, lane(k)] = state_row(arrived, half, i + 4, k)
             to_prev[8 * i : 8 * i + 8, lane(k)] = state_row(arrived, half, i, k)
     if half:
+        head = refs[0]
+        for q in range(3):
+            to_next[STATE + 4 * q : STATE + 4 * q + 4, :] = head[16 * q : 16 * q + 4, :]
+            to_prev[STATE + 4 * q : STATE + 4 * q + 4, :] = head[16 * q + 12 : 16 * q + 16, :]
         return
+    head = refs[0]
     for n in range(SLABS):
         for core in range(2):
             base = (2 * n + core) * CHUNK + 32
@@ -130,33 +135,33 @@
             while j < 6 * n + 6:
                 stop = min(6 * n + 6, j // 8 * 8 + 8)
                 q, k, x = j // 32, j % 32 // 8, j % 8
-                piece = arrived[base + j - 6 * n : base + stop - 6 * n, :]
-                at = STATE + 16 * q + 8 * core + x
-                to_next[at : at + stop - j, lane(k)] = piece
-                to_prev[at : at + stop - j, lane(k)] = piece
+                at = 16 * q + 8 * core + x
+                head[at : at + stop - j, lane(k)] = arrived[base + j - 6 * n : base + stop - 6 * n, :]
                 j = stop
     for core in range(2):
         for group in range(2):
             start = (16 * group + core) * CHUNK + 38
-            piece = arrived[pl.ds(start, 8, stride=2 * CHUNK), :]
-            at = STATE + 48
-            to_next[at : at + 8, lane(2 * group + core)] = piece
-            to_prev[at : at + 8, lane(2 * group + core)] = piece
+            head[48:56, lane(2 * group + core)] = arrived[pl.ds(start, 8, stride=2 * CHUNK), :]
+    for q in range(3):
+        at = STATE + REACH * q
+        to_next[at : at + REACH, :] = head[16 * q + 4 : 16 * q + 16, :]
+        to_prev[at : at + REACH, :] = head[16 * q : 16 * q + REACH, :]
+    for ref in (to_next, to_prev):
+        ref[FIRST - 8 : FIRST, :] = head[48:56, :]
 
 
 def next_offset(n):
-    return 8 + sum(15 - m for m in range(n // 8 * 8, n))
+    return 8 + sum(15 - m for m in range(n))
 
 
 def prev_offset(n):
-    return sum(15 - m for m in range(n + 1, n // 8 * 8 + 8))
+    return sum(15 - m for m in range(n + 1, 15))
 
 
 def fine_kernel(half, arrived, mine, low_head, high_head, low, high, *refs):
-    field, other, coarse, wx, kk, ax, axw, py, my, pq, mq, steps, frac = refs[-13:]
+    field, other, coarse, wx, kk, ax, axw, wy, ay, steps, frac = refs[-11:]
     for tile in range(6):
-        ref = (low_head, mine, high_head)[tile // 2]
-        at = STATE + 48
+        ref, at = ((low_head, FIRST - 8), (mine, 48), (high_head, FIRST - 8))[tile // 2]
         number = ref[at : at + 8, lane(2 * half + tile % 2)]
         steps[tile] = number
         frac[tile] = 1.0 / jnp.maximum(number, 1.0)
@@ -164,7 +169,7 @@
     def limited(size, half_fraction):
         return size * (0.5 - half_fraction * size)
 
-    def set_up(head, states, first, groups, row):
+    def set_up(head, states, first, groups, row, step):
         def group_rows(i, carry):
             group = first + i
             r = 4 * group + 2
@@ -178,32 +183,25 @@
                 else:
                     field[r + j] = states[pl.ds(pl.multiple_of(32 * i + 8 * j, 8), 8), :]
                 east, north, spread = [
-                    jnp.broadcast_to(head[pl.ds(STATE + 16 * q + row + 4 * i + j, 1), :], (8, Y))
+                    jnp.broadcast_to(head[pl.ds(row + step * q + 4 * i + j, 1), :], (8, Y))
                     for q in range(3)
                 ]
                 wx[r + j] = east
                 kk[r + j] = spread
                 ax[r + j] = limited(jnp.abs(east), half_fraction)
-                south = join(from_left(split(north)))
-                forward, backward = jnp.maximum(north, 0.0), jnp.minimum(south, 0.0)
-                py[r + j] = forward
-                my[r + j] = backward
-                pq[r + j] = limited(forward, half_fraction)
-                mq[r + j] = limited(-backward, half_fraction)
+                wy[r + j] = north
+                ay[r + j] = limited(jnp.abs(north), half_fraction)
             return carry
 
         lax.fori_loop(0, groups, group_rows, 0)
 
-    set_up(low_head, low, 0, REACH // 4, ROWS - REACH)
-    set_up(mine, None, REACH // 4, ROWS // 4, 0)
-    set_up(high_head, high, (REACH + ROWS) // 4, REACH // 4, 0)
+    set_up(low_head, low, 0, REACH // 4, STATE, REACH)
+    set_up(mine, None, REACH // 4, ROWS // 4, 0, ROWS)
+    set_up(high_head, high, (REACH + ROWS) // 4, REACH // 4, STATE, REACH)
 
     def flux(w, a, here, there, slope_here, slope_there):
         up = w > 0.0
         return w * jnp.where(up, here, there) + a * jnp.where(up, slope_here, slope_there)
-
-    def outgoing(a, b, value, slope):
-        return a * value + b * slope
 
     def block(substep, source, target, index):
         r = 4 * index + 2
@@ -225,18 +223,16 @@
                 west = each(flux, split(wx[r + i - 1]), a, c[i - 1], c[i], sx[i - 1], sx[i])
             a = split(ax[r + i])
             east = each(flux, split(wx[r + i]), a, c[i], c[i + 1], sx[i], sx[i + 1])
-            dy = minus(from_right(c[i]), c[i])
+            right = from_right(c[i])
+            dy = minus(right, c[i])
             dy_left = minus(c[i], from_left(c[i]))
             sy = each(minmod, dy, dy_left)
-            north = each(outgoing, split(py[r + i]), split(pq[r + i]), c[i], sy)
-            south = each(outgoing, split(my[r + i]), split(mq[r + i]), c[i], sy)
-            north_left = from_left(north)
-            south_right = from_right(south)
+            north = each(flux, split(wy[r + i]), split(ay[r + i]), c[i], right, sy, from_right(sy))
+            south = from_left(north)
             k_row = split(kk[r + i])
             for p in range(PIECES):
                 spread = (dx[i][p] - dx[i - 1][p]) + (dy[p] - dy_left[p])
-                along = (north_left[p] - north[p]) + (south[p] - south_right[p])
-                rate = (west[p] - east[p]) + along + k_row[p] * spread
+                rate = (west[p] - east[p]) + (south[p] - north[p]) + k_row[p] * spread
                 target[r + i, :, lane(p)] = c[i][p] + active[i // 4] * rate
 
     def upwind(w, here, there):
@@ -249,17 +245,13 @@
         for j in range(4):
             right = from_right(c[j])
             left = from_left(c[j])
-            north = each(lambda a, b: a * b, split(py[r + j]), c[j])
-            south = each(lambda a, b: a * b, split(my[r + j]), c[j])
-            north_left = from_left(north)
-            south_right = from_right(south)
+            north = each(upwind, split(wy[r + j]), c[j], right)
+            south = from_left(north)
             k_row = split(kk[r + j])
             for p in range(PIECES):
                 spread = c[j - 1][p] + c[j + 1][p] + left[p] + right[p] - 4.0 * c[j][p]
-                along = (north_left[p] - north[p]) + (south[p] - south_right[p])
-                coarse[4 * index + j, :, lane(p)] = (
-                    c[j][p] + (fx[j][p] - fx[j + 1][p]) + along + k_row[p] * spread
-                )
+                along = (fx[j][p] - fx[j + 1][p]) + (south[p] - north[p])
+                coarse[4 * index + j, :, lane(p)] = c[j][p] + along + k_row[p] * spread
         return carry
 
     lax.fori_loop(0, ROWS // 4, coarse_rows, 0)
@@ -298,12 +290,9 @@
 
 
 def pack(half, out, to_next, to_prev):
-    base = WIDE_HALO * half
-    to_next[base : base + 8, :] = jnp.zeros((8, Y), WIDE)
-    used = next_offset(8 * half + 7) + 8 - 8 * half
-    total = NARROW_HALO if half else WIDE_HALO
-    for ref, filled in ((to_next, used), (to_prev, used - 8)):
-        ref[base + filled : base + total, :] = jnp.zeros((total - filled, Y), WIDE)
+    if half == 0:
+        to_next[0:8, :] = jnp.zeros((8, Y), WIDE)
+        to_prev[HALO - 8 : HALO, :] = jnp.zeros((8, Y), WIDE)
     for n in range(8 * half, min(8 * half + 8, 15)):
         rows = 15 - n
         for k in range(PIECES):
@@ -312,13 +301,13 @@
                 at = (2 * (n - 8 * half) + upper) * 32 + 8 * k
                 return out[at + first : at + last, :]
 
-            at = base + next_offset(n)
+            at = next_offset(n)
             if rows > 8:
                 to_next[at : at + rows - 8, lane(k)] = piece(16 - rows, 8, 0)
                 to_next[at + rows - 8 : at + rows, lane(k)] = piece(0, 8, 1)
             else:
                 to_next[at : at + rows, lane(k)] = piece(8 - rows, 8, 1)
-            at = base + prev_offset(n)
+            at = prev_offset(n)
             if rows > 8:
                 to_prev[at : at + 8, lane(k)] = piece(0, 8, 0)
                 to_prev[at + 8 : at + rows, lane(k)] = piece(0, rows - 8, 1)
@@ -351,15 +340,14 @@
 
 def differences(half, n, own, low, high):
     size = 8 if half else 16
-    base = WIDE_HALO * half
     tiles = []
     if n < 15:
-        at = base + next_offset(n) + 15 - n - size
+        at = next_offset(n) + 15 - n - size
         tiles += [rows_at(low, at + 8 * k) for k in range(size // 8)]
     at = 16 * (n - 8 * half)
     tiles += [rows_at(own, at), rows_at(own, at + 8)]
     if n < 15:
-        at = base + prev_offset(n)
+        at = prev_offset(n)
         tiles += [rows_at(high, at + 8 * k) for k in range(size // 8)]
     return tiles
 
@@ -385,13 +373,21 @@
     return result
 
 
-def chain_kernel(own, later, mine, low_head, high_head, low, high, out, stencil):
+def chain_kernel(own, later, mine, *refs):
+    low_a, high_a, low_b, high_b, low, high, out, stencil, edge = refs
     inside = jnp.where(lax.axis_index("z") < CHIPS - 1, 1.0, 0.0).astype(WIDE)
+
+    for q in range(3):
+        edge[0, 16 * q : 16 * q + 4, :] = low_b[STATE + 4 * q : STATE + 4 * q + 4, :]
+        edge[1, 16 * q + 12 : 16 * q + 16, :] = high_b[STATE + 4 * q : STATE + 4 * q + 4, :]
+        at = STATE + REACH * q
+        edge[0, 16 * q + 4 : 16 * q + 16, :] = low_a[at : at + REACH, :]
+        edge[1, 16 * q : 16 * q + REACH, :] = high_a[at : at + REACH, :]
 
     def rows_of(q):
         return [
-            rows_at(ref, STATE + 16 * q + 8 * upper)
-            for ref in (low_head, mine, high_head)
+            rows_at(ref, 16 * q + 8 * upper)
+            for ref in (edge.at[0], mine, edge.at[1])
             for upper in range(2)
         ]
 
@@ -463,14 +459,13 @@
     arrived = lax.all_to_all(sent, ("slab", "core"), 0, 0, tiled=True)
     arrived = arrived.reshape(TR * LEV * CHUNK, LANE)
 
-    head = STATE + 56
-    next_a, prev_a = call(functools.partial(arrange_kernel, 0), [(head, Y), (head, Y)], "v")(
-        arrived
-    )
+    mine, next_a, prev_a = call(
+        functools.partial(arrange_kernel, 0), [(56, Y), (FIRST, Y), (FIRST, Y)], "v"
+    )(arrived)
     low_a, high_a = to_chip(next_a, 1), to_chip(prev_a, -1)
     next_b, prev_b = call(
-        functools.partial(arrange_kernel, 1), [(STATE, Y), (STATE, Y)], "vh"
-    )(arrived, next_a)
+        functools.partial(arrange_kernel, 1), [(REST, Y), (REST, Y)], "vv"
+    )(arrived, mine)
     low_b, high_b = to_chip(next_b, 1), to_chip(prev_b, -1)
 
     rows = pltpu.VMEM((EXT + 4, 8, Y), WIDE)
@@ -482,8 +477,6 @@
         rows,
         rows,
         pltpu.VMEM((EXT // 4, 8, Y), WIDE),
-        rows,
-        rows,
         rows,
         rows,
         pltpu.VMEM((6, 8, LANE), WIDE),
@@ -496,8 +489,8 @@
         scratch=scratch,
         flops=25000000,
         nbytes=3000000,
-    )(arrived, next_a, low_a, high_a, low_a, high_a)
-    halo = (WIDE_HALO + NARROW_HALO, Y)
+    )(arrived, mine, low_a, high_a, low_a, high_a)
+    halo = (HALO, Y)
     own_b, next_c, prev_c = call(
         functools.partial(fine_kernel, 1),
         [(512, LANE), halo, halo],
@@ -505,15 +498,15 @@
         scratch=scratch,
         flops=25000000,
         nbytes=3000000,
-    )(arrived, next_a, low_a, high_a, low_b, high_b, own_a)
+    )(arrived, mine, low_a, high_a, low_b, high_b, own_a)
     low_c, high_c = to_chip(next_c, 1), to_chip(prev_c, -1)
     (chain,) = call(
         chain_kernel,
         [(256, Y)],
-        "vvvvvvv",
-        scratch=[pltpu.VMEM((5, 48, Y), WIDE)],
+        "vvvvvvvvv",
+        scratch=[pltpu.VMEM((5, 48, Y), WIDE), pltpu.VMEM((2, 48, Y), WIDE)],
         flops=8000000,
-    )(from_tiles(own_a), from_tiles(own_b), next_a, low_a, high_a, low_c, high_c)
+    )(from_tiles(own_a), from_tiles(own_b), mine, low_a, high_a, low_b, high_b, low_c, high_c)
     result = lax.all_to_all(
         chain.reshape(SLABS * 2, 8, Y), ("slab", "core"), 0, 0, tiled=True
     )

time: 88.3 us -> 87.2 us (0.988)
  the two profiles are of different devices: /device:TPU:225 before, /device:TPU:97 now
where the time goes in v4:
time: 87.2 us; the launch traced here: 86.9 us
  blocking collectives  37.5 us (43%)
  Pallas kernels  19.2 us (22%)
  starting transfers between devices  18.5 us (21%)
  waiting for transfers between devices  10.1 us (12%)
    all_to_all x1, blocking collectives, on_device(): arrived = lax.all_to_all(sent, ('slab', 'core'), 0, 0, tiled=True)  20.7 us
    ppermute x6, starting transfers between devices, to_chip(): return lax.ppermute(array, AXES, route)  18.5 us
    all_to_all x1, blocking collectives, on_device(): lax.all_to_all(chain.reshape(SLABS * 2, 8, Y), ('slab', 'core'), 0, 0, ti...  16.8 us
    ppermute x6, waiting for transfers between devices, to_chip(): return lax.ppermute(array, AXES, route)  10.1 us
    pallas_call x1, Pallas kernels, on_device(): call(functools.partial(fine_kernel, 1), [(512, LANE), halo, halo], 'vvvvv...  7.84 us
    pallas_call x1, Pallas kernels, on_device(): call(functools.partial(fine_kernel, 0), [(512, LANE)], 'vvvvvv', scratch=...  7.76 us
    pallas_call x1, Pallas kernels, on_device(): call(prepare_kernel, [(TR * LEV, CHUNK, LANE)], 'hhhhh', scratch=[pltpu.V...  2.11 us
  transfers between devices with their start and end apart: 6, of which 3 were waited for; matrix products, arithmetic and copies ran while one was open for 0% of the time, Pallas kernels for 9%

profile of v4, /device:TPU:97, one launch (start us, length us, event | category | flops | bytes accessed | tf_op | source)
XLA Modules:
  0.0 86.9 jit_solution(6724150831809731679)
XLA Ops:
  0.7 2.1 %shard_map.55 = f32[32,40,128]{2,1,0:T(8,128)} custom-call(s32[1,1]{1,0:T(1,128)S(6)} %copy.7.count_ref, f32[32,32,128]{2,1,0:T(8,128)} %bitcast.41, f32[8,32,128]{2,1,0:T(8,128)} %bitcast.42, f32[8,32,128]{2,1,0:T(8,128)} %bitcast.43, f32[8,32,128]{2,1,0:T(8,128)} %bitcast.44), custom_call_target="tpu_custom_call" | custom-call | flops 300000 | bytes 2000000 | tf_op jit(solution)/shard_map/pallas_call | solution.py:446
  2.8 20.7 %all_to_all.10 = f32[32,40,128]{2,1,0:T(8,128)S(1)} all-to-all(f32[32,40,128]{2,1,0:T(8,128)} %shard_map.55), channel_id=1, replica_groups=mesh['slab'=16,'z'=16,'core'=2] {'slab','core'}, dimensions={0} | all-to-all | bytes 1310720 | tf_op jit(solution)/shard_map/all_to_all | solution.py:459
  23.5 0.1 shard_map.56
  23.6 4.8 %collective-permute-start = (f32[140,512]{1,0:T(8,128)S(1)}, f32[140,512]{1,0:T(8,128)S(1)}, u32[]{:S(2)}, u32[]{:S(2)}) collective-permute-start(f32[140,512]{1,0:T(8,128)S(1)} %get-tuple-element.14), channel_id=1, source_target_pairs={{0,2},{1,3},{2,4},{3,5},{4,6},{5,7},{6,8},{7,9},{8,10},{9,11},{10,... | collective-permute-start | bytes 860168 | tf_op jit(solution)/shard_map/ppermute | solution.py:437
  28.4 1.9 %collective-permute-start.1 = (f32[140,512]{1,0:T(8,128)S(1)}, f32[140,512]{1,0:T(8,128)S(1)}, u32[]{:S(2)}, u32[]{:S(2)}) collective-permute-start(f32[140,512]{1,0:T(8,128)S(1)} %get-tuple-element.15), channel_id=1, source_target_pairs={{2,0},{3,1},{4,2},{5,3},{6,4},{7,5},{8,6},{9,7},{10,8},{11,9},{12,... | collective-permute-start | bytes 860168 | tf_op jit(solution)/shard_map/ppermute | solution.py:437
  30.3 0.1 shard_map.58
  30.4 4.6 %collective-permute-start.2 = (f32[108,512]{1,0:T(8,128)S(1)}, f32[108,512]{1,0:T(8,128)S(1)}, u32[]{:S(2)}, u32[]{:S(2)}) collective-permute-start(f32[108,512]{1,0:T(8,128)S(1)} %get-tuple-element.16), channel_id=1, source_target_pairs={{0,2},{1,3},{2,4},{3,5},{4,6},{5,7},{6,8},{7,9},{8,10},{9,11},{10,... | collective-permute-start | bytes 663560 | tf_op jit(solution)/shard_map/ppermute | solution.py:437
  35.0 1.9 %collective-permute-start.3 = (f32[108,512]{1,0:T(8,128)S(1)}, f32[108,512]{1,0:T(8,128)S(1)}, u32[]{:S(2)}, u32[]{:S(2)}) collective-permute-start(f32[108,512]{1,0:T(8,128)S(1)} %get-tuple-element.17), channel_id=1, source_target_pairs={{2,0},{3,1},{4,2},{5,3},{6,4},{7,5},{8,6},{9,7},{10,8},{11,9},{12,... | collective-permute-start | bytes 663560 | tf_op jit(solution)/shard_map/ppermute | solution.py:437
  36.9 0.0 collective-permute-done.low_head.low.refs_0_
  36.9 3.1 %collective-permute-done.1.high_head.high.refs_1_ = f32[140,512]{1,0:T(8,128)S(1)} collective-permute-done((f32[140,512]{1,0:T(8,128)S(1)}, f32[140,512]{1,0:T(8,128)S(1)}, u32[]{:S(2)}, u32[]{:S(2)}) %collective-permute-start.1) | collective-permute-done | bytes 286752 | tf_op jit(solution)/shard_map/ppermute | solution.py:437
  40.0 7.8 %shard_map.57.refs_0_ = f32[512,128]{1,0:T(8,128)S(1)} custom-call(f32[1280,128]{1,0:T(8,128)S(1)} %bitcast.35, f32[56,512]{1,0:T(8,128)S(1)} %get-tuple-element.13.mine.refs_0_, f32[140,512]{1,0:T(8,128)S(1)} %collective-permute-done.low_head.low.refs_0_, f32[140,512]{1,0:T(8,128)S(1)} %collective-permute-done.1.high_head.high.refs_1_, ...), custom_call_target="tpu_custom_call" | custom-call | flops 25000000 | bytes 3000000 | tf_op jit(solution)/shard_map/pallas_call | solution.py:485
  47.8 0.0 collective-permute-done.2.low.refs_2_
  47.8 0.0 collective-permute-done.3.high.refs_3_
  47.8 7.8 %shard_map.59 = (f32[512,128]{1,0:T(8,128)S(1)}, f32[128,512]{1,0:T(8,128)S(1)}, f32[128,512]{1,0:T(8,128)S(1)}) custom-call(f32[1280,128]{1,0:T(8,128)S(1)} %bitcast.36, f32[56,512]{1,0:T(8,128)S(1)} %get-tuple-element.13.mine.refs_0_, f32[140,512]{1,0:T(8,128)S(1)} %collective-permute-done.low_head.low.refs_0_, ...), custom_call_target="tpu_custom_call" | custom-call | flops 25000000 | bytes 3000000 | tf_op jit(solution)/shard_map/pallas_call | solution.py:494
  55.7 2.7 %collective-permute-start.4 = (f32[128,512]{1,0:T(8,128)S(1)}, f32[128,512]{1,0:T(8,128)S(1)}, u32[]{:S(2)}, u32[]{:S(2)}) collective-permute-start(f32[128,512]{1,0:T(8,128)S(1)} %get-tuple-element.19), channel_id=1, source_target_pairs={{0,2},{1,3},{2,4},{3,5},{4,6},{5,7},{6,8},{7,9},{8,10},{9,11},{10,... | collective-permute-start | bytes 786440 | tf_op jit(solution)/shard_map/ppermute | solution.py:437
  58.4 2.6 %collective-permute-start.5 = (f32[128,512]{1,0:T(8,128)S(1)}, f32[128,512]{1,0:T(8,128)S(1)}, u32[]{:S(2)}, u32[]{:S(2)}) collective-permute-start(f32[128,512]{1,0:T(8,128)S(1)} %get-tuple-element.20), channel_id=1, source_target_pairs={{2,0},{3,1},{4,2},{5,3},{6,4},{7,5},{8,6},{9,7},{10,8},{11,9},{12,... | collective-permute-start | bytes 786440 | tf_op jit(solution)/shard_map/ppermute | solution.py:437
  61.0 3.5 %collective-permute-done.4.refs_4_ = f32[128,512]{1,0:T(8,128)S(1)} collective-permute-done((f32[128,512]{1,0:T(8,128)S(1)}, f32[128,512]{1,0:T(8,128)S(1)}, u32[]{:S(2)}, u32[]{:S(2)}) %collective-permute-start.4) | collective-permute-done | bytes 262176 | tf_op jit(solution)/shard_map/ppermute | solution.py:437
  64.5 3.5 %collective-permute-done.5.refs_5_ = f32[128,512]{1,0:T(8,128)S(1)} collective-permute-done((f32[128,512]{1,0:T(8,128)S(1)}, f32[128,512]{1,0:T(8,128)S(1)}, u32[]{:S(2)}, u32[]{:S(2)}) %collective-permute-start.5) | collective-permute-done | bytes 262176 | tf_op jit(solution)/shard_map/ppermute | solution.py:437
  68.0 1.2 %shard_map.60 = f32[256,512]{1,0:T(8,128)S(1)} custom-call(f32[128,512]{1,0:T(8,128)S(1)} %bitcast.37, f32[128,512]{1,0:T(8,128)S(1)} %bitcast.39, f32[56,512]{1,0:T(8,128)S(1)} %get-tuple-element.13.mine.refs_0_, f32[140,512]{1,0:T(8,128)S(1)} %collective-permute-done.low_head.low.refs_0_, f32[140,512]{1,0:T(8,128)S(1)} %collective-permute-done.1.high_head.high.refs_1_, ...), custom_call_target="tpu_custom_call" | custom-call | flops 8000000 | bytes 1000000 | tf_op jit(solution)/shard_map/pallas_call | solution.py:503
  69.3 16.8 %all_to_all.11 = f32[32,8,512]{2,1,0:T(8,128)S(1)} all-to-all(f32[32,8,512]{2,1,0:T(8,128)S(1)} %bitcast.38), channel_id=1, replica_groups=mesh['slab'=16,'z'=16,'core'=2] {'slab','core'}, dimensions={0} | all-to-all | bytes 1048576 | tf_op jit(solution)/shard_map/all_to_all | solution.py:510
  86.1 0.8 copy.8
Async XLA Ops:
  23.6 13.3 %collective-permute-start = (f32[140,512]{1,0:T(8,128)S(1)}, f32[140,512]{1,0:T(8,128)S(1)}, u32[]{:S(2)}, u32[]{:S(2)}) collective-permute-start(f32[140,512]{1,0:T(8,128)S(1)} %get-tuple-element.14), channel_id=1, source_target_pairs={{0,2},{1,3},{2,4},{3,5},{4,6},{5,7},{6,8},{7,9},{8,10},{9,11},{10,... | collective-permute-start | bytes 860168 | tf_op jit(solution)/shard_map/ppermute | solution.py:437
  28.4 11.7 %collective-permute-start.1 = (f32[140,512]{1,0:T(8,128)S(1)}, f32[140,512]{1,0:T(8,128)S(1)}, u32[]{:S(2)}, u32[]{:S(2)}) collective-permute-start(f32[140,512]{1,0:T(8,128)S(1)} %get-tuple-element.15), channel_id=1, source_target_pairs={{2,0},{3,1},{4,2},{5,3},{6,4},{7,5},{8,6},{9,7},{10,8},{11,9},{12,... | collective-permute-start | bytes 860168 | tf_op jit(solution)/shard_map/ppermute | solution.py:437
  30.4 17.4 %collective-permute-start.2 = (f32[108,512]{1,0:T(8,128)S(1)}, f32[108,512]{1,0:T(8,128)S(1)}, u32[]{:S(2)}, u32[]{:S(2)}) collective-permute-start(f32[108,512]{1,0:T(8,128)S(1)} %get-tuple-element.16), channel_id=1, source_target_pairs={{0,2},{1,3},{2,4},{3,5},{4,6},{5,7},{6,8},{7,9},{8,10},{9,11},{10,... | collective-permute-start | bytes 663560 | tf_op jit(solution)/shard_map/ppermute | solution.py:437
  35.0 12.8 %collective-permute-start.3 = (f32[108,512]{1,0:T(8,128)S(1)}, f32[108,512]{1,0:T(8,128)S(1)}, u32[]{:S(2)}, u32[]{:S(2)}) collective-permute-start(f32[108,512]{1,0:T(8,128)S(1)} %get-tuple-element.17), channel_id=1, source_target_pairs={{2,0},{3,1},{4,2},{5,3},{6,4},{7,5},{8,6},{9,7},{10,8},{11,9},{12,... | collective-permute-start | bytes 663560 | tf_op jit(solution)/shard_map/ppermute | solution.py:437
  55.7 8.8 %collective-permute-start.4 = (f32[128,512]{1,0:T(8,128)S(1)}, f32[128,512]{1,0:T(8,128)S(1)}, u32[]{:S(2)}, u32[]{:S(2)}) collective-permute-start(f32[128,512]{1,0:T(8,128)S(1)} %get-tuple-element.19), channel_id=1, source_target_pairs={{0,2},{1,3},{2,4},{3,5},{4,6},{5,7},{6,8},{7,9},{8,10},{9,11},{10,... | collective-permute-start | bytes 786440 | tf_op jit(solution)/shard_map/ppermute | solution.py:437
  58.4 9.6 %collective-permute-start.5 = (f32[128,512]{1,0:T(8,128)S(1)}, f32[128,512]{1,0:T(8,128)S(1)}, u32[]{:S(2)}, u32[]{:S(2)}) collective-permute-start(f32[128,512]{1,0:T(8,128)S(1)} %get-tuple-element.20), channel_id=1, source_target_pairs={{2,0},{3,1},{4,2},{5,3},{6,4},{7,5},{8,6},{9,7},{10,8},{11,9},{12,... | collective-permute-start | bytes 786440 | tf_op jit(solution)/shard_map/ppermute | solution.py:437

commit v5 on v4

--- a/solution.py
+++ b/solution.py
@@ -18,7 +18,7 @@
 EXT = ROWS + 2 * REACH
 CHUNK = 40
 STATE = 8 * REACH
-FIRST, REST, HALO = STATE + 3 * REACH + 8, STATE + 3 * (ROWS - REACH), 128
+FIRST, REST, HALO = STATE + 3 * REACH + 8, STATE + 3 * (ROWS - REACH), 120
 WIDE = jnp.float32
 AXES = ("slab", "z", "core")
 
@@ -151,7 +151,7 @@
 
 
 def next_offset(n):
-    return 8 + sum(15 - m for m in range(n))
+    return sum(15 - m for m in range(n))
 
 
 def prev_offset(n):
@@ -290,9 +290,6 @@
 
 
 def pack(half, out, to_next, to_prev):
-    if half == 0:
-        to_next[0:8, :] = jnp.zeros((8, Y), WIDE)
-        to_prev[HALO - 8 : HALO, :] = jnp.zeros((8, Y), WIDE)
     for n in range(8 * half, min(8 * half + 8, 15)):
         rows = 15 - n
         for k in range(PIECES):
@@ -338,17 +335,23 @@
     return split(ref[at : at + 8, :])
 
 
+def rows_inside(ref, at):
+    begin = min(max(at, 0), HALO - 8)
+    tile = rows_at(ref, begin)
+    return [pltpu.roll(part, (begin - at) % 8, 0) for part in tile] if begin != at else tile
+
+
 def differences(half, n, own, low, high):
     size = 8 if half else 16
     tiles = []
     if n < 15:
         at = next_offset(n) + 15 - n - size
-        tiles += [rows_at(low, at + 8 * k) for k in range(size // 8)]
+        tiles += [rows_inside(low, at + 8 * k) for k in range(size // 8)]
     at = 16 * (n - 8 * half)
     tiles += [rows_at(own, at), rows_at(own, at + 8)]
     if n < 15:
         at = prev_offset(n)
-        tiles += [rows_at(high, at + 8 * k) for k in range(size // 8)]
+        tiles += [rows_inside(high, at + 8 * k) for k in range(size // 8)]
     return tiles
 
 

time: 87.2 us -> 86.9 us (level)
  no operation moved by 1% of the time
where the time goes in v5:
time: 86.9 us; the launch traced here: 86.5 us
  blocking collectives  37.5 us (43%)
  Pallas kernels  19.2 us (22%)
  starting transfers between devices  18.5 us (21%)
  waiting for transfers between devices  9.79 us (11%)
    all_to_all x1, blocking collectives, on_device(): arrived = lax.all_to_all(sent, ('slab', 'core'), 0, 0, tiled=True)  20.7 us
    ppermute x6, starting transfers between devices, to_chip(): return lax.ppermute(array, AXES, route)  18.5 us
    all_to_all x1, blocking collectives, on_device(): lax.all_to_all(chain.reshape(SLABS * 2, 8, Y), ('slab', 'core'), 0, 0, ti...  16.8 us
    ppermute x6, waiting for transfers between devices, to_chip(): return lax.ppermute(array, AXES, route)  9.79 us
    pallas_call x1, Pallas kernels, on_device(): call(functools.partial(fine_kernel, 1), [(512, LANE), halo, halo], 'vvvvv...  7.84 us
    pallas_call x1, Pallas kernels, on_device(): call(functools.partial(fine_kernel, 0), [(512, LANE)], 'vvvvvv', scratch=...  7.76 us
    pallas_call x1, Pallas kernels, on_device(): call(prepare_kernel, [(TR * LEV, CHUNK, LANE)], 'hhhhh', scratch=[pltpu.V...  2.11 us
  transfers between devices with their start and end apart: 6, of which 3 were waited for; matrix products, arithmetic and copies ran while one was open for 0% of the time, Pallas kernels for 9%

profile of v5, /device:TPU:97, one launch (start us, length us, event | category | flops | bytes accessed | tf_op | source)
XLA Modules:
  0.0 86.5 jit_solution(7223465992915243536)
XLA Ops:
  0.7 2.1 %shard_map.55 = f32[32,40,128]{2,1,0:T(8,128)} custom-call(s32[1,1]{1,0:T(1,128)S(6)} %copy.7.count_ref, f32[32,32,128]{2,1,0:T(8,128)} %bitcast.41, f32[8,32,128]{2,1,0:T(8,128)} %bitcast.42, f32[8,32,128]{2,1,0:T(8,128)} %bitcast.43, f32[8,32,128]{2,1,0:T(8,128)} %bitcast.44), custom_call_target="tpu_custom_call" | custom-call | flops 300000 | bytes 2000000 | tf_op jit(solution)/shard_map/pallas_call | solution.py:449
  2.8 20.7 %all_to_all.10 = f32[32,40,128]{2,1,0:T(8,128)S(1)} all-to-all(f32[32,40,128]{2,1,0:T(8,128)} %shard_map.55), channel_id=1, replica_groups=mesh['slab'=16,'z'=16,'core'=2] {'slab','core'}, dimensions={0} | all-to-all | bytes 1310720 | tf_op jit(solution)/shard_map/all_to_all | solution.py:462
  23.5 0.1 shard_map.56
  23.6 4.8 %collective-permute-start = (f32[140,512]{1,0:T(8,128)S(1)}, f32[140,512]{1,0:T(8,128)S(1)}, u32[]{:S(2)}, u32[]{:S(2)}) collective-permute-start(f32[140,512]{1,0:T(8,128)S(1)} %get-tuple-element.14), channel_id=1, source_target_pairs={{0,2},{1,3},{2,4},{3,5},{4,6},{5,7},{6,8},{7,9},{8,10},{9,11},{10,... | collective-permute-start | bytes 860168 | tf_op jit(solution)/shard_map/ppermute | solution.py:440
  28.4 1.9 %collective-permute-start.1 = (f32[140,512]{1,0:T(8,128)S(1)}, f32[140,512]{1,0:T(8,128)S(1)}, u32[]{:S(2)}, u32[]{:S(2)}) collective-permute-start(f32[140,512]{1,0:T(8,128)S(1)} %get-tuple-element.15), channel_id=1, source_target_pairs={{2,0},{3,1},{4,2},{5,3},{6,4},{7,5},{8,6},{9,7},{10,8},{11,9},{12,... | collective-permute-start | bytes 860168 | tf_op jit(solution)/shard_map/ppermute | solution.py:440
  30.3 0.1 shard_map.58
  30.4 4.6 %collective-permute-start.2 = (f32[108,512]{1,0:T(8,128)S(1)}, f32[108,512]{1,0:T(8,128)S(1)}, u32[]{:S(2)}, u32[]{:S(2)}) collective-permute-start(f32[108,512]{1,0:T(8,128)S(1)} %get-tuple-element.16), channel_id=1, source_target_pairs={{0,2},{1,3},{2,4},{3,5},{4,6},{5,7},{6,8},{7,9},{8,10},{9,11},{10,... | collective-permute-start | bytes 663560 | tf_op jit(solution)/shard_map/ppermute | solution.py:440
  35.0 1.9 %collective-permute-start.3 = (f32[108,512]{1,0:T(8,128)S(1)}, f32[108,512]{1,0:T(8,128)S(1)}, u32[]{:S(2)}, u32[]{:S(2)}) collective-permute-start(f32[108,512]{1,0:T(8,128)S(1)} %get-tuple-element.17), channel_id=1, source_target_pairs={{2,0},{3,1},{4,2},{5,3},{6,4},{7,5},{8,6},{9,7},{10,8},{11,9},{12,... | collective-permute-start | bytes 663560 | tf_op jit(solution)/shard_map/ppermute | solution.py:440
  36.9 0.0 collective-permute-done.low_head.low.refs_0_
  36.9 3.1 %collective-permute-done.1.high_head.high.refs_1_ = f32[140,512]{1,0:T(8,128)S(1)} collective-permute-done((f32[140,512]{1,0:T(8,128)S(1)}, f32[140,512]{1,0:T(8,128)S(1)}, u32[]{:S(2)}, u32[]{:S(2)}) %collective-permute-start.1) | collective-permute-done | bytes 286752 | tf_op jit(solution)/shard_map/ppermute | solution.py:440
  40.0 7.8 %shard_map.57.refs_0_ = f32[512,128]{1,0:T(8,128)S(1)} custom-call(f32[1280,128]{1,0:T(8,128)S(1)} %bitcast.35, f32[56,512]{1,0:T(8,128)S(1)} %get-tuple-element.13.mine.refs_0_, f32[140,512]{1,0:T(8,128)S(1)} %collective-permute-done.low_head.low.refs_0_, f32[140,512]{1,0:T(8,128)S(1)} %collective-permute-done.1.high_head.high.refs_1_, ...), custom_call_target="tpu_custom_call" | custom-call | flops 25000000 | bytes 3000000 | tf_op jit(solution)/shard_map/pallas_call | solution.py:488
  47.8 0.0 collective-permute-done.2.low.refs_2_
  47.8 0.0 collective-permute-done.3.high.refs_3_
  47.8 7.8 %shard_map.59 = (f32[512,128]{1,0:T(8,128)S(1)}, f32[120,512]{1,0:T(8,128)S(1)}, f32[120,512]{1,0:T(8,128)S(1)}) custom-call(f32[1280,128]{1,0:T(8,128)S(1)} %bitcast.36, f32[56,512]{1,0:T(8,128)S(1)} %get-tuple-element.13.mine.refs_0_, f32[140,512]{1,0:T(8,128)S(1)} %collective-permute-done.low_head.low.refs_0_, ...), custom_call_target="tpu_custom_call" | custom-call | flops 25000000 | bytes 3000000 | tf_op jit(solution)/shard_map/pallas_call | solution.py:497
  55.7 2.7 %collective-permute-start.4 = (f32[120,512]{1,0:T(8,128)S(1)}, f32[120,512]{1,0:T(8,128)S(1)}, u32[]{:S(2)}, u32[]{:S(2)}) collective-permute-start(f32[120,512]{1,0:T(8,128)S(1)} %get-tuple-element.19), channel_id=1, source_target_pairs={{0,2},{1,3},{2,4},{3,5},{4,6},{5,7},{6,8},{7,9},{8,10},{9,11},{10,... | collective-permute-start | bytes 737288 | tf_op jit(solution)/shard_map/ppermute | solution.py:440
  58.4 2.6 %collective-permute-start.5 = (f32[120,512]{1,0:T(8,128)S(1)}, f32[120,512]{1,0:T(8,128)S(1)}, u32[]{:S(2)}, u32[]{:S(2)}) collective-permute-start(f32[120,512]{1,0:T(8,128)S(1)} %get-tuple-element.20), channel_id=1, source_target_pairs={{2,0},{3,1},{4,2},{5,3},{6,4},{7,5},{8,6},{9,7},{10,8},{11,9},{12,... | collective-permute-start | bytes 737288 | tf_op jit(solution)/shard_map/ppermute | solution.py:440
  61.0 3.2 %collective-permute-done.4.refs_4_ = f32[120,512]{1,0:T(8,128)S(1)} collective-permute-done((f32[120,512]{1,0:T(8,128)S(1)}, f32[120,512]{1,0:T(8,128)S(1)}, u32[]{:S(2)}, u32[]{:S(2)}) %collective-permute-start.4) | collective-permute-done | bytes 245792 | tf_op jit(solution)/shard_map/ppermute | solution.py:440
  64.2 3.5 %collective-permute-done.5.refs_5_ = f32[120,512]{1,0:T(8,128)S(1)} collective-permute-done((f32[120,512]{1,0:T(8,128)S(1)}, f32[120,512]{1,0:T(8,128)S(1)}, u32[]{:S(2)}, u32[]{:S(2)}) %collective-permute-start.5) | collective-permute-done | bytes 245792 | tf_op jit(solution)/shard_map/ppermute | solution.py:440
  67.7 1.2 %shard_map.60 = f32[256,512]{1,0:T(8,128)S(1)} custom-call(f32[128,512]{1,0:T(8,128)S(1)} %bitcast.37, f32[128,512]{1,0:T(8,128)S(1)} %bitcast.39, f32[56,512]{1,0:T(8,128)S(1)} %get-tuple-element.13.mine.refs_0_, f32[140,512]{1,0:T(8,128)S(1)} %collective-permute-done.low_head.low.refs_0_, f32[140,512]{1,0:T(8,128)S(1)} %collective-permute-done.1.high_head.high.refs_1_, ...), custom_call_target="tpu_custom_call" | custom-call | flops 8000000 | bytes 1000000 | tf_op jit(solution)/shard_map/pallas_call | solution.py:506
  68.9 16.8 %all_to_all.11 = f32[32,8,512]{2,1,0:T(8,128)S(1)} all-to-all(f32[32,8,512]{2,1,0:T(8,128)S(1)} %bitcast.38), channel_id=1, replica_groups=mesh['slab'=16,'z'=16,'core'=2] {'slab','core'}, dimensions={0} | all-to-all | bytes 1048576 | tf_op jit(solution)/shard_map/all_to_all | solution.py:513
  85.7 0.8 copy.8
Async XLA Ops:
  23.6 13.3 %collective-permute-start = (f32[140,512]{1,0:T(8,128)S(1)}, f32[140,512]{1,0:T(8,128)S(1)}, u32[]{:S(2)}, u32[]{:S(2)}) collective-permute-start(f32[140,512]{1,0:T(8,128)S(1)} %get-tuple-element.14), channel_id=1, source_target_pairs={{0,2},{1,3},{2,4},{3,5},{4,6},{5,7},{6,8},{7,9},{8,10},{9,11},{10,... | collective-permute-start | bytes 860168 | tf_op jit(solution)/shard_map/ppermute | solution.py:440
  28.4 11.7 %collective-permute-start.1 = (f32[140,512]{1,0:T(8,128)S(1)}, f32[140,512]{1,0:T(8,128)S(1)}, u32[]{:S(2)}, u32[]{:S(2)}) collective-permute-start(f32[140,512]{1,0:T(8,128)S(1)} %get-tuple-element.15), channel_id=1, source_target_pairs={{2,0},{3,1},{4,2},{5,3},{6,4},{7,5},{8,6},{9,7},{10,8},{11,9},{12,... | collective-permute-start | bytes 860168 | tf_op jit(solution)/shard_map/ppermute | solution.py:440
  30.4 17.4 %collective-permute-start.2 = (f32[108,512]{1,0:T(8,128)S(1)}, f32[108,512]{1,0:T(8,128)S(1)}, u32[]{:S(2)}, u32[]{:S(2)}) collective-permute-start(f32[108,512]{1,0:T(8,128)S(1)} %get-tuple-element.16), channel_id=1, source_target_pairs={{0,2},{1,3},{2,4},{3,5},{4,6},{5,7},{6,8},{7,9},{8,10},{9,11},{10,... | collective-permute-start | bytes 663560 | tf_op jit(solution)/shard_map/ppermute | solution.py:440
  35.0 12.8 %collective-permute-start.3 = (f32[108,512]{1,0:T(8,128)S(1)}, f32[108,512]{1,0:T(8,128)S(1)}, u32[]{:S(2)}, u32[]{:S(2)}) collective-permute-start(f32[108,512]{1,0:T(8,128)S(1)} %get-tuple-element.17), channel_id=1, source_target_pairs={{2,0},{3,1},{4,2},{5,3},{6,4},{7,5},{8,6},{9,7},{10,8},{11,9},{12,... | collective-permute-start | bytes 663560 | tf_op jit(solution)/shard_map/ppermute | solution.py:440
  55.7 8.5 %collective-permute-start.4 = (f32[120,512]{1,0:T(8,128)S(1)}, f32[120,512]{1,0:T(8,128)S(1)}, u32[]{:S(2)}, u32[]{:S(2)}) collective-permute-start(f32[120,512]{1,0:T(8,128)S(1)} %get-tuple-element.19), channel_id=1, source_target_pairs={{0,2},{1,3},{2,4},{3,5},{4,6},{5,7},{6,8},{7,9},{8,10},{9,11},{10,... | collective-permute-start | bytes 737288 | tf_op jit(solution)/shard_map/ppermute | solution.py:440
  58.4 9.3 %collective-permute-start.5 = (f32[120,512]{1,0:T(8,128)S(1)}, f32[120,512]{1,0:T(8,128)S(1)}, u32[]{:S(2)}, u32[]{:S(2)}) collective-permute-start(f32[120,512]{1,0:T(8,128)S(1)} %get-tuple-element.20), channel_id=1, source_target_pairs={{2,0},{3,1},{4,2},{5,3},{6,4},{7,5},{8,6},{9,7},{10,8},{11,9},{12,... | collective-permute-start | bytes 737288 | tf_op jit(solution)/shard_map/ppermute | solution.py:440
